TPU v7x, 32 devices: a whole 2x2x4 slice. The times are simulated.
32 devices in a mesh: win: 2 (over y), chan: 16 (over z, x, core), tm: 1.
Axes of the slice: x: 2, y: 2, z: 4, core: 2. Of those that a mesh axis runs over, the one named last changes fastest.
Arguments:
- records: float32 [1024, 32768], P(('win', 'chan'), 'tm'), parts along dimension 0, may hold values from -1000 to 1000
- dead_mask: int32 [1024], P(('win', 'chan')), parts along dimension 0, may hold values 0 or 1
- offsets: int32 [16], P('win'), parts along dimension 0, may hold values from 0 to 511, as said below
Outputs:
- correlations: bfloat16 [32, 1024, 256], P('tm', ('win', 'chan')), parts along dimension 1
There are 2 independent parts, one for each index of `win`. A program takes and returns all parts, laid end to end along the dimension named above; each array names one. Nothing has to cross between parts.
Inputs may be any that keep to these rules, and one draw needn't show every extreme that they name: `dead_mask`: 1 marks a dead channel. Window w begins at sample w * 4096 + offsets[w]; some window has offset 512 - 1.
All inputs are finite; a program needn't handle non-finite values. No bound on the sum of `dead_mask` on one device may be relied on, other than what follows from the above.
Results may differ from a plain program's by a relative error of at most 0.0033.
Values may be sent and summed in bfloat16 or wider, within the bound.
No kernel may reach another device: no remote copies, remote signals or barrier semaphores. Data moves between devices by JAX's collectives and lax.ppermute only.
A program may use at most 64 MiB of HBM per device.

v0:
```python
import functools
import math

import jax
import jax.numpy as jnp
import ml_dtypes
import numpy as np
from jax import lax
from jax.experimental import pallas as pl
from jax.experimental.pallas import tpu as pltpu
from jax.sharding import PartitionSpec as P

L = 8192
HOP = 4096
H = 128
K0 = 32
NF = 256
WB = 64
NLAG = 32
NPART = 256
EDGE = 512
STEP = 256
GROUP = 512
EPS = 1e-05
TWO_PI = 2.0 * math.pi
BF16 = jnp.bfloat16
F32 = jnp.float32


def split_table(table):
    high = table.astype(ml_dtypes.bfloat16)
    low = (table - high.astype(np.float64)).astype(ml_dtypes.bfloat16)
    return high, low


@functools.cache
def fourier_tables():
    samples = np.arange(GROUP)[:, None]
    bins = K0 + np.arange(NF)[None, :]
    angle = (samples * bins % L) * (TWO_PI / L)
    inner = np.concatenate([np.cos(angle), -np.sin(angle)], axis=1)
    outer = np.zeros((GROUP, 128))
    for lane, k, wave in ((0, K0 - 1, np.cos), (64, K0 - 1, np.sin), (127, K0 + NF, np.cos), (63, K0 + NF, np.sin)):
        sign = 1.0 if wave is np.cos else -1.0
        outer[:, lane] = sign * wave((samples[:, 0] * k % L) * (TWO_PI / L))
    high, low = split_table(inner)
    return np.concatenate([high, outer.astype(ml_dtypes.bfloat16)], axis=1), low


@functools.cache
def packed_tables():
    return np.concatenate(fourier_tables(), axis=1)


@functools.cache
def lag_tables():
    lags = np.arange(NLAG)[:, None] - NLAG // 2
    angle = (lags * (K0 + np.arange(NF))[None, :] % L) * (TWO_PI / L)
    return np.cos(angle).astype(np.float32), np.sin(angle).astype(np.float32)


def split(value):
    high = value.astype(BF16)
    return high, (value - high.astype(F32)).astype(BF16)


def inverse(value):
    guess = pl.reciprocal(value, approx=True)
    return guess * (2.0 - value * guess)


def dot(a, b):
    return jnp.dot(a, b, preferred_element_type=F32)


def spectra_kernel(
    halves, own, halo,
    dead, offs, x_hbm, table_hbm, out, x, absolute, norm_high, norm_low, parts, table, sems,
):
    channels = x.shape[0]
    groups = HOP // GROUP
    bulk = min(own + 1, halves)
    edges = min(own + 2, halves)
    width = halves * HOP
    middle = HOP // 2 + H
    firsts, seconds = [], []
    for j in range(halves):
        firsts.append((j * HOP - (H if j or halo else 0), j * HOP + middle))
        seconds.append((j * HOP + middle, (j + 1) * HOP - H if j + 1 < halves else width + halo))
    copies = [
        pltpu.make_async_copy(
            x_hbm.at[:, pl.ds(halo + begin, end - begin)], x.at[:, pl.ds(H + begin, end - begin)],
            sems.at[i],
        )
        for i, (begin, end) in enumerate(firsts + seconds)
    ]
    table_copy = pltpu.make_async_copy(table_hbm, table, sems.at[2 * halves])
    for copy in copies[:halves] + [table_copy] + copies[halves:]:
        copy.start()
    if not halo:
        for begin in (0, H + width):
            absolute[:, begin:begin + H] = jnp.zeros((channels, H), BF16)

    def arrive(ids):
        for i in ids:
            copies[i].wait()
        for i in ids:
            begin, end = (firsts + seconds)[i]
            here = slice(H + begin, H + end)
            absolute[:, here] = jnp.abs(x[:, here]).astype(BF16)

    high = table.at[:, :2 * NF + 128]
    low = table.at[:, 2 * NF + 128:]
    from_lane = lax.broadcasted_iota(jnp.int32, (2 * H + STEP, STEP), 0)
    to_lane = lax.broadcasted_iota(jnp.int32, (2 * H + STEP, STEP), 1)
    level_band = ((from_lane >= to_lane) & (from_lane <= to_lane + 2 * H)).astype(F32).astype(BF16)
    from_bin = lax.broadcasted_iota(jnp.int32, (NF, NF), 0)
    to_bin = lax.broadcasted_iota(jnp.int32, (NF, NF), 1)
    smooth_band = (jnp.abs(from_bin - to_bin) <= WB).astype(F32).astype(BF16)
    lane = lax.broadcasted_iota(jnp.int32, (1, parts.shape[1]), 1)
    outer_place = lane - 2 * NF
    outer_first = (outer_place == 0) | (outer_place == 64)
    every_bin = jnp.where(
        lane < 2 * NF, jnp.bitwise_and(lane, NF - 1) + K0, jnp.where(outer_first, K0 - 1, K0 + NF)
    )
    real_place = (lane < NF) | (outer_place == 0) | (outer_place == 127)
    group = lax.broadcasted_iota(jnp.int32, (groups, 1), 0) * GROUP
    angle = jnp.bitwise_and(group * every_bin, L - 1).astype(F32) * (TWO_PI / L)
    turn_same = jnp.cos(angle)
    turn_swap = jnp.sin(angle) * jnp.where(real_place, -1.0, 1.0)
    bin_index = lax.broadcasted_iota(jnp.int32, (1, NF), 1)
    below, above = jnp.minimum(bin_index, WB), jnp.minimum(NF - 1 - bin_index, WB)
    inverse_count = 1.0 / (below + above + 1).astype(F32)

    def rows(ref, begin, length, count):
        return [ref[:, begin + j * HOP:begin + j * HOP + length] for j in range(count)]

    def store(place, value):
        here = slice(place, place + value.shape[0])
        norm_high[here, :], norm_low[here, :] = split(value)

    def normalise(group_ids, place):
        blocks = [(g, g * GROUP + part * STEP) for g in group_ids for part in range(GROUP // STEP)]
        counts = [edges if g == 0 else bulk for g, _ in blocks]
        level = dot(
            jnp.concatenate(
                [r for (_, begin), n in zip(blocks, counts)
                 for r in rows(absolute, begin, STEP + 2 * H, n)], axis=0
            ), level_band,
        ) * (1.0 / (2 * H + 1)) + EPS
        values = []
        at = 0
        for (_, begin), n in zip(blocks, counts):
            samples = jnp.concatenate(rows(x, H + begin, STEP, n), axis=0)
            values.append(samples * inverse(level[at:at + n * channels]))
            at += n * channels
        begins = {}
        for index, g in enumerate(group_ids):
            value = jnp.concatenate(values[2 * index:2 * index + 2], axis=1)
            if g == 0:
                lane = lax.broadcasted_iota(jnp.int32, (channels, EDGE), 1)
                merged = []
                for w in range(own):
                    mine = value[w * channels:(w + 1) * channels]
                    other = (
                        value[(w + 2) * channels:(w + 3) * channels]
                        if w + 2 < edges else jnp.zeros_like(mine)
                    )
                    merged.append(jnp.where(lane >= offs[w], mine, other))
                begins["edge"] = place
                store(place, jnp.concatenate(merged, axis=0))
                place += own * channels
                value = value[:bulk * channels]
            begins[g] = place
            store(place, value)
            place += bulk * channels
        return begins, place

    def transform(begin, end):
        first = dot(norm_high[begin:end, :], high[...])
        second = dot(norm_low[begin:end, :], high[:, :2 * NF])
        second = second + dot(norm_high[begin:end, :], low[...])
        parts[begin:end, :2 * NF] = first[:, :2 * NF] + second
        parts[begin:end, 2 * NF:] = first[:, 2 * NF:]

    begins = {}
    place = 0
    waiting = None
    arrive(range(halves))
    table_copy.wait()
    for g in range(0, groups, 2):
        if g == groups // 2:
            arrive(range(halves, 2 * halves))
        start = place
        found, place = normalise([g, g + 1], place)
        begins.update(found)
        if waiting:
            transform(*waiting)
        waiting = (start, place)
    transform(*waiting)

    def piece(name, j):
        return parts[begins[name] + j * channels:begins[name] + (j + 1) * channels, :]

    def bulk_of(j):
        same = jnp.zeros((channels, parts.shape[1]), F32)
        swap = same
        for g in range(1, groups):
            value = piece(g, j)
            same = same + value * turn_same[g:g + 1, :]
            swap = swap + value * turn_swap[g:g + 1, :]
        return same + jnp.concatenate(
            [swap[:, NF:2 * NF], swap[:, :NF], pltpu.roll(swap[:, 2 * NF:], 64, 1)], axis=1
        )

    window = lax.broadcasted_iota(jnp.int32, (own, 1), 0)
    offsets = sum(jnp.where(window == w, offs[w], 0) for w in range(own))
    lane = lax.broadcasted_iota(jnp.int32, (1, NF), 1)
    outer_lane = lax.broadcasted_iota(jnp.int32, (1, 128), 1)
    outer_bin = jnp.where((outer_lane == 0) | (outer_lane == 64), K0 - 1, K0 + NF)

    def turn(bins):
        angle = jnp.bitwise_and(bins * offsets, L - 1).astype(F32) * (TWO_PI / L)
        return jnp.cos(angle), jnp.sin(angle)

    cos_turn, sin_turn = turn(lane + K0)
    cos_outer, sin_outer = turn(outer_bin)
    sign = 1.0 - 2.0 * jnp.bitwise_and(lane + K0, 1).astype(F32)
    sign_outer = 1.0 - 2.0 * jnp.bitwise_and(outer_bin, 1).astype(F32)
    channel = lax.broadcasted_iota(jnp.int32, (channels, 1), 0)
    live = 1.0 - sum(jnp.where(channel == i, dead[i], 0) for i in range(channels)).astype(F32)

    signs = jnp.concatenate([sign, sign, sign_outer], axis=1)
    reals, imags, magnitudes = [], [], []
    following = bulk_of(0)
    for w in range(own):
        spec = following + piece("edge", w)
        if w + 1 < bulk:
            following = bulk_of(w + 1)
            spec = spec + (following + piece(0, w + 1)) * signs
        spec = spec * live
        outer = spec[:, 2 * NF:]
        c, s = cos_turn[w:w + 1], sin_turn[w:w + 1]
        c_outer, s_outer = cos_outer[w:w + 1], sin_outer[w:w + 1]
        outer_imag = pltpu.roll(outer, 64, 1)

        def hann(inner, ends):
            ends = jnp.concatenate([ends, ends], axis=1)
            before = jnp.where(lane == 0, ends, pltpu.roll(inner, 1, 1))
            behind = jnp.where(lane == NF - 1, ends, pltpu.roll(inner, NF - 1, 1))
            return 0.5 * inner - 0.25 * (before + behind)

        real = hann(
            spec[:, :NF] * c - spec[:, NF:2 * NF] * s, outer * c_outer - outer_imag * s_outer
        )
        imag = hann(
            spec[:, :NF] * s + spec[:, NF:2 * NF] * c, outer * s_outer + outer_imag * c_outer
        )
        reals.append(real)
        imags.append(imag)
        magnitudes.append(jnp.sqrt(real * real + imag * imag + 1e-12))
    m_high, m_low = split(jnp.concatenate(magnitudes, axis=0))
    smooth = (dot(m_high, smooth_band) + dot(m_low, smooth_band)) * inverse_count
    scale = 1.0 / (smooth + EPS)
    flip = flip_matrix(channels)
    for w in range(own):
        here = slice(w * channels, (w + 1) * channels)
        white = jnp.concatenate([reals[w] * scale[here], imags[w] * scale[here]], axis=1)
        out[:, w * 2 * NF:(w + 1) * 2 * NF] = dot(flip, white.astype(BF16)).astype(BF16)


def flip_matrix(channels):
    row = lax.broadcasted_iota(jnp.int32, (channels, channels), 0)
    column = lax.broadcasted_iota(jnp.int32, (channels, channels), 1)
    return (row + column == channels - 1).astype(F32).astype(BF16)


def rotate_kernel(lags, own, cos_lag, sin_lag, out):
    channels = own.shape[0]
    straight = dot(flip_matrix(channels), own[...])
    real, imag = straight[:, :NF], straight[:, NF:]
    for t in range(lags):
        c, s = cos_lag[t:t + 1, :], sin_lag[t:t + 1, :]
        here = slice(t * channels, (t + 1) * channels)
        out[here, :NF] = (real * c - imag * s).astype(BF16)
        out[here, NF:] = (real * s + imag * c).astype(BF16)


def put_slots(channels, partners, present, absent):
    last = NPART // channels - 1
    nothing = jnp.zeros((channels, partners.shape[1]), BF16)

    def place(slot):
        return pl.ds(pl.multiple_of((last - slot) * channels, channels), channels)

    for block, slot, valid in present:
        partners[place(slot), :] = block[...]

        @pl.when(jnp.logical_not(valid))
        def _(slot=slot):
            partners[place(slot), :] = nothing

    for slot in absent:
        partners[place(slot), :] = nothing


def early_slots(me, count, channels, blocks, partners):
    own, ahead = blocks
    next_level = me // 4 + 1 < count // 4
    put_slots(
        channels, partners, [(own, 0, me >= 0), (ahead, 4, next_level)], (1, 2, 3, 5, 6, 7)
    )


def late_slots(me, count, channels, blocks, partners):
    core = lax.rem(me, 2)
    side = lax.rem(me // 2, 2)
    (own_swapped, ahead_swapped, far, far_swapped, cross, cross_swapped, other,
     other_swapped) = blocks
    cross_slot = 6 - 4 * side
    other_slot = 8 - cross_slot
    step = 1 - 2 * core
    next_level = me // 4 + 1 < count // 4
    second_level = me // 4 + 2 < count // 4
    other_there = (side == 0) | second_level
    put_slots(channels, partners, [
        (far, 0, second_level), (cross, cross_slot, next_level),
        (other, other_slot, other_there), (ahead_swapped, 4 + step, next_level),
        (cross_swapped, cross_slot + step, next_level),
        (other_swapped, other_slot + step, other_there),
    ], (4,))

    @pl.when(core == 0)
    def _():
        put_slots(channels, partners, [(own_swapped, 1, me >= 0)], ())

    @pl.when(core == 1)
    def _():
        put_slots(channels, partners, [(far_swapped, 7, second_level)], ())


def product_kernel(late, count, norm_scale, place, rotated, *refs):
    refs = list(refs)
    before = refs.pop(0) if late else None
    out, partners, total = refs[-3:]
    blocks = refs[:-3]
    channels = blocks[0].shape[0]
    (late_slots if late else early_slots)(place[0], count, channels, blocks, partners)
    rows, features = rotated.shape
    chunk = 2 * 2 * NF
    for begin in range(0, features, chunk):
        turned = partners[:, begin:begin + chunk].T
        product = dot(rotated[:, begin:begin + chunk], turned)
        if begin == 0:
            total[...] = product
        else:
            total[...] += product

    row = lax.broadcasted_iota(jnp.int32, (channels, NPART), 0)
    column = lax.broadcasted_iota(jnp.int32, (channels, NPART), 1)
    low = row + column >= NPART - 1
    keep = (low | (column < NPART - channels)) if late else jnp.logical_not(low)
    sheared = []
    for begin in range(0, rows, channels):
        here = slice(begin, begin + channels)
        value = jnp.where(keep, total[here, :], 0.0)
        if late:
            value = (value + before[here, :]) * norm_scale
            sheared.append(pltpu.roll(value, 1, 1, stride=1, stride_axis=0).astype(BF16))
        else:
            out[here, :] = value
    if late:
        sheared = jnp.concatenate(sheared, axis=0)
        out[...] = dot(sheared, flip_matrix(NPART)).astype(BF16)


def exchange(value, pairs):
    return lax.ppermute(value, "chan", pairs)


def local(records, dead_mask, offsets):
    channels, samples = records.shape
    tm_count = lax.axis_size("tm")
    tm_index = lax.axis_index("tm")
    chan_count = lax.axis_size("chan")
    own = samples // HOP
    windows = own * tm_count
    halves = own
    halo = 0
    if tm_count > 1:
        reach = 2 * HOP + H
        left = lax.ppermute(
            records[:, samples - H:], "tm", [(i, i + 1) for i in range(tm_count - 1)]
        )
        right = lax.ppermute(
            records[:, :reach], "tm", [(i + 1, i) for i in range(tm_count - 1)]
        )
        records = jnp.concatenate([left, records, right], axis=1)
        halves = own + 2
        halo = H
    table = jnp.asarray(packed_tables())
    own_offsets = lax.dynamic_slice_in_dim(offsets, tm_index * own, own, 0)
    vmem = pl.BlockSpec(memory_space=pltpu.VMEM)
    smem = pl.BlockSpec(memory_space=pltpu.SMEM)
    hbm = pl.BlockSpec(memory_space=pl.ANY)
    params = pltpu.CompilerParams(vmem_limit_bytes=24 * 1024 * 1024)

    bulk = min(own + 1, halves)
    part_rows = (own + bulk * (HOP // GROUP)) * channels
    spectra = pl.pallas_call(
        functools.partial(spectra_kernel, halves, own, halo),
        name="spectra",
        out_shape=jax.ShapeDtypeStruct((channels, own * 2 * NF), BF16),
        in_specs=[smem, smem, hbm, hbm],
        out_specs=vmem,
        scratch_shapes=[
            pltpu.VMEM((channels, halves * HOP + 2 * H), F32),
            pltpu.VMEM((channels, halves * HOP + 2 * H), BF16),
            pltpu.VMEM((part_rows, GROUP), BF16),
            pltpu.VMEM((part_rows, GROUP), BF16),
            pltpu.VMEM((part_rows, 2 * NF + 128), F32),
            pltpu.VMEM(table.shape, BF16),
            pltpu.SemaphoreType.DMA((2 * halves + 1,)),
        ],
        compiler_params=pltpu.CompilerParams(vmem_limit_bytes=60 * 1024 * 1024),
        cost_estimate=pl.CostEstimate(
            flops=7_000_000_000, bytes_accessed=8 * 1024 * 1024, transcendentals=0
        ),
    )(dead_mask, own_offsets, records, table)
    if tm_count > 1:
        spectra = lax.all_gather(spectra, "tm", axis=1, tiled=True)

    lags = NLAG // tm_count
    cos_lag, sin_lag = (
        lax.dynamic_slice_in_dim(jnp.asarray(t), tm_index * lags, lags, 0) for t in lag_tables()
    )
    place = lax.axis_index("chan").astype(jnp.int32).reshape(1)
    norm_scale = 1.0 / math.sqrt(2.0 * NF * windows)

    features = spectra.shape[1]
    rotated = pl.pallas_call(
        functools.partial(rotate_kernel, lags),
        name="rotate",
        grid=(windows,),
        out_shape=jax.ShapeDtypeStruct((lags * channels, features), BF16),
        in_specs=[
            pl.BlockSpec((channels, 2 * NF), lambda w: (0, w)),
            pl.BlockSpec((lags, NF), lambda w: (0, 0)),
            pl.BlockSpec((lags, NF), lambda w: (0, 0)),
        ],
        out_specs=pl.BlockSpec((lags * channels, 2 * NF), lambda w: (0, w)),
        compiler_params=params,
        cost_estimate=pl.CostEstimate(
            flops=4_000_000_000, bytes_accessed=8 * 1024 * 1024, transcendentals=0
        ),
    )(spectra, cos_lag, sin_lag)

    def product(blocks, before):
        late = before is not None
        operands = [place, rotated] + ([before] if late else []) + list(blocks)
        return pl.pallas_call(
            functools.partial(product_kernel, late, chan_count, norm_scale),
            name="late_product" if late else "early_product",
            out_shape=jax.ShapeDtypeStruct((lags * channels, NPART), BF16 if late else F32),
            in_specs=[smem] + [vmem] * (len(operands) - 1),
            out_specs=vmem,
            scratch_shapes=[
                pltpu.VMEM((NPART, features), BF16),
                pltpu.VMEM((lags * channels, NPART), F32),
            ],
            compiler_params=params,
            cost_estimate=pl.CostEstimate(
                flops=2 * lags * channels * features * NPART, bytes_accessed=6 * 1024 * 1024,
                transcendentals=0,
            ),
        )(*operands)

    every = range(chan_count)
    down = [(i, (i - 4) % chan_count) for i in every]
    down_2 = [(i, (i - 2) % chan_count) for i in every]
    across = [(i, i ^ 2) for i in every]
    cores = [(i, i ^ 1) for i in every]
    side = lax.rem(lax.axis_index("chan") // 2, 2)

    ahead = exchange(spectra, down)
    ahead, rotated = lax.optimization_barrier((ahead, rotated))
    cross = exchange(ahead, across)
    other = exchange(jnp.where(side == 0, ahead, spectra), down_2)
    far = exchange(ahead, down)
    early = product((spectra, ahead), None)
    kept, ahead, cross, early = lax.optimization_barrier((spectra, ahead, cross, early))
    own_swapped = exchange(kept, cores)
    ahead_swapped = exchange(ahead, cores)
    other_swapped = exchange(other, cores)
    far, other_swapped, own_swapped, ahead_swapped = lax.optimization_barrier(
        (far, other_swapped, own_swapped, ahead_swapped)
    )
    blocks = (own_swapped, ahead_swapped, far, exchange(far, cores), cross,
              exchange(cross, cores), other, other_swapped)
    return product(blocks, early).reshape(lags, channels, NPART)


def solution(mesh):
    return jax.shard_map(
        local,
        mesh=mesh,
        in_specs=(P(("win", "chan"), "tm"), P(("win", "chan")), P("win")),
        out_specs=P("tm", ("win", "chan"), None),
        check_vma=False,
    )
```

profile of v0, /device:TPU:0, one launch (start us, length us, event | category | flops | bytes accessed | tf_op | source)
XLA Modules:
  0.0 43.5 jit_solution(12662664435568483573)
XLA Ops:
  0.0 0.0 copy-start.2
  0.0 0.0 copy-start.3
  0.0 11.5 %spectra.1.own.refs_0_ = bf16[32,4096]{1,0:T(8,128)(2,1)} custom-call(s32[32]{0:T(128)} %dead.1, s32[8]{0:T(128)} %offs, f32[32,32768]{1,0:T(8,128)} %x_hbm.1, bf16[512,1152]{1,0:T(8,128)(2,1)} %constant.30.clone.table_hbm), custom_call_target="tpu_custom_call" | custom-call | flops 7000000000 | bytes 8388608 | tf_op jit(solution)/shard_map/spectra/pallas_call | solution.py:410
  11.6 5.1 %collective-permute-start = (bf16[32,4096]{1,0:T(8,128)(2,1)}, bf16[32,4096]{1,0:T(8,128)(2,1)S(1)}, u32[]{:S(2)}, u32[]{:S(2)}) collective-permute-start(bf16[32,4096]{1,0:T(8,128)(2,1)} %spectra.1.own.refs_0_), channel_id=1, source_target_pairs={{0,12},{1,13},{2,14},{3,15},{4,0},{5,1},{6,2},{7,3},{8,4},{9,5},{1... | collective-permute-start | bytes 786440 | tf_op jit(solution)/shard_map/ppermute | solution.py:378
  16.7 0.0 copy-done.2
  16.7 0.0 copy-done.3
  16.7 0.0 copy-start
  16.7 1.0 %copy-done = bf16[32,4096]{1,0:T(8,128)(2,1)S(1)} copy-done((bf16[32,4096]{1,0:T(8,128)(2,1)S(1)}, bf16[32,4096]{1,0:T(8,128)(2,1)}, u32[]{:S(2)}) %copy-start) | copy-done | bytes 262168
  17.6 0.0 copy-start.1
  17.6 3.7 %rotate.1.rotated = bf16[1024,4096]{1,0:T(8,128)(2,1)S(1)} custom-call(bf16[32,4096]{1,0:T(8,128)(2,1)S(1)} %copy-done, f32[32,256]{1,0:T(8,128)S(1)} %copy-done.3, f32[32,256]{1,0:T(8,128)S(1)} %copy-done.2), custom_call_target="tpu_custom_call" | custom-call | flops 4000000000 | bytes 8388608 | tf_op jit(solution)/shard_map/rotate/pallas_call | solution.py:441
  21.3 1.2 %collective-permute-done.refs_1_ = bf16[32,4096]{1,0:T(8,128)(2,1)S(1)} collective-permute-done((bf16[32,4096]{1,0:T(8,128)(2,1)}, bf16[32,4096]{1,0:T(8,128)(2,1)S(1)}, u32[]{:S(2)}, u32[]{:S(2)}) %collective-permute-start) | collective-permute-done | bytes 262176 | tf_op jit(solution)/shard_map/ppermute | solution.py:378
  22.5 1.5 %collective-permute-start.1 = (bf16[32,4096]{1,0:T(8,128)(2,1)S(1)}, bf16[32,4096]{1,0:T(8,128)(2,1)S(1)}, u32[]{:S(2)}, u32[]{:S(2)}) collective-permute-start(bf16[32,4096]{1,0:T(8,128)(2,1)S(1)} %collective-permute-done.refs_1_), channel_id=1, source_target_pairs={{0,2},{1,3},{2,0},{3,1},{4,6},{5,7},{6,4},{7,5},{8,10},{9,11},{10,... | collective-permute-start | bytes 786440 | tf_op jit(solution)/shard_map/ppermute | solution.py:378
  24.1 4.2 %collective-permute-start.3 = (bf16[32,4096]{1,0:T(8,128)(2,1)S(1)}, bf16[32,4096]{1,0:T(8,128)(2,1)S(1)}, u32[]{:S(2)}, u32[]{:S(2)}) collective-permute-start(bf16[32,4096]{1,0:T(8,128)(2,1)S(1)} %broadcast_select_fusion), channel_id=1, source_target_pairs={{0,14},{1,15},{2,0},{3,1},{4,2},{5,3},{6,4},{7,5},{8,6},{9,7},{10,... | collective-permute-start | bytes 786440 | tf_op jit(solution)/shard_map/ppermute | solution.py:378
  28.3 0.1 collective-permute-start.2
  28.3 0.0 copy-done.1
  28.4 2.4 %early_product.1.refs_0_ = f32[1024,256]{1,0:T(8,128)S(1)} custom-call(s32[1]{0:T(128)} %bitcast.place, bf16[1024,4096]{1,0:T(8,128)(2,1)S(1)} %rotate.1.rotated, bf16[32,4096]{1,0:T(8,128)(2,1)S(1)} %copy-done.1, bf16[32,4096]{1,0:T(8,128)(2,1)S(1)} %collective-permute-done.refs_1_), custom_call_target="tpu_custom_call" | custom-call | flops 2147483648 | bytes 6291456 | tf_op jit(solution)/shard_map/early_product/pallas_call | solution.py:461
  30.7 3.6 %collective-permute-done.1.refs_5_ = bf16[32,4096]{1,0:T(8,128)(2,1)S(1)} collective-permute-done((bf16[32,4096]{1,0:T(8,128)(2,1)S(1)}, bf16[32,4096]{1,0:T(8,128)(2,1)S(1)}, u32[]{:S(2)}, u32[]{:S(2)}) %collective-permute-start.1) | collective-permute-done | bytes 262176 | tf_op jit(solution)/shard_map/ppermute | solution.py:378
  34.3 0.0 collective-permute-start.5
  34.3 1.0 %collective-permute-done.3.refs_7_ = bf16[32,4096]{1,0:T(8,128)(2,1)S(1)} collective-permute-done((bf16[32,4096]{1,0:T(8,128)(2,1)S(1)}, bf16[32,4096]{1,0:T(8,128)(2,1)S(1)}, u32[]{:S(2)}, u32[]{:S(2)}) %collective-permute-start.3) | collective-permute-done | bytes 262176 | tf_op jit(solution)/shard_map/ppermute | solution.py:378
  35.3 0.0 collective-permute-start.4
  35.3 0.5 %collective-permute-start.6 = (bf16[32,4096]{1,0:T(8,128)(2,1)S(1)}, bf16[32,4096]{1,0:T(8,128)(2,1)S(1)}, u32[]{:S(2)}, u32[]{:S(2)}) collective-permute-start(bf16[32,4096]{1,0:T(8,128)(2,1)S(1)} %collective-permute-done.refs_1_), channel_id=1, source_target_pairs={{0,1},{1,0},{2,3},{3,2},{4,5},{5,4},{6,7},{7,6},{8,9},{9,8},{10,11... | collective-permute-start | bytes 786440 | tf_op jit(solution)/shard_map/ppermute | solution.py:378
  35.8 0.0 collective-permute-start.8
  35.8 2.4 %collective-permute-done.2.refs_3_ = bf16[32,4096]{1,0:T(8,128)(2,1)S(1)} collective-permute-done((bf16[32,4096]{1,0:T(8,128)(2,1)S(1)}, bf16[32,4096]{1,0:T(8,128)(2,1)S(1)}, u32[]{:S(2)}, u32[]{:S(2)}) %collective-permute-start.2) | collective-permute-done | bytes 262176 | tf_op jit(solution)/shard_map/ppermute | solution.py:378
  38.3 0.0 collective-permute-done.4.refs_8_
  38.3 0.0 collective-permute-done.5.refs_1_
  38.3 0.0 collective-permute-done.6.refs_2_
  38.3 0.1 collective-permute-start.7
  38.4 0.0 collective-permute-done.8.refs_6_
  38.4 1.5 %collective-permute-done.7.refs_4_ = bf16[32,4096]{1,0:T(8,128)(2,1)S(1)} collective-permute-done((bf16[32,4096]{1,0:T(8,128)(2,1)S(1)}, bf16[32,4096]{1,0:T(8,128)(2,1)S(1)}, u32[]{:S(2)}, u32[]{:S(2)}) %collective-permute-start.7) | collective-permute-done | bytes 262176 | tf_op jit(solution)/shard_map/ppermute | solution.py:378
  39.9 3.6 %late_product.1 = bf16[1024,256]{1,0:T(8,128)(2,1)} custom-call(s32[1]{0:T(128)} %bitcast.place, bf16[1024,4096]{1,0:T(8,128)(2,1)S(1)} %rotate.1.rotated, f32[1024,256]{1,0:T(8,128)S(1)} %early_product.1.refs_0_, bf16[32,4096]{1,0:T(8,128)(2,1)S(1)} %collective-permute-done.5.refs_1_, bf16[32,4096]{1,0:T(8,128)(2,1)S(1)} %collective-permute-done.6.refs_2_, ...), custom_call_target="tpu_custom_call" | custom-call | flops 2147483648 | bytes 6291456 | tf_op jit(solution)/shard_map/late_product/pallas_call | solution.py:461
  (1 shorter events, 0.0 us)
Async XLA Ops:
  0.0 16.7 %copy-start.2 = (f32[32,256]{1,0:T(8,128)S(1)}, f32[32,256]{1,0:T(8,128)}, u32[]{:S(2)}) copy-start(f32[32,256]{1,0:T(8,128)} %constant.32.clone.sin_lag) | copy-start | bytes 98308
  0.0 16.7 %copy-start.3 = (f32[32,256]{1,0:T(8,128)S(1)}, f32[32,256]{1,0:T(8,128)}, u32[]{:S(2)}) copy-start(f32[32,256]{1,0:T(8,128)} %constant.31.clone.cos_lag) | copy-start | bytes 98308
  11.6 11.0 %collective-permute-start = (bf16[32,4096]{1,0:T(8,128)(2,1)}, bf16[32,4096]{1,0:T(8,128)(2,1)S(1)}, u32[]{:S(2)}, u32[]{:S(2)}) collective-permute-start(bf16[32,4096]{1,0:T(8,128)(2,1)} %spectra.1.own.refs_0_), channel_id=1, source_target_pairs={{0,12},{1,13},{2,14},{3,15},{4,0},{5,1},{6,2},{7,3},{8,4},{9,5},{1... | collective-permute-start | bytes 786440 | tf_op jit(solution)/shard_map/ppermute | solution.py:378
  16.7 1.0 %copy-start = (bf16[32,4096]{1,0:T(8,128)(2,1)S(1)}, bf16[32,4096]{1,0:T(8,128)(2,1)}, u32[]{:S(2)}) copy-start(bf16[32,4096]{1,0:T(8,128)(2,1)} %spectra.1.own.refs_0_) | copy-start | bytes 786436
  17.6 10.7 %copy-start.1 = (bf16[32,4096]{1,0:T(8,128)(2,1)S(1)}, bf16[32,4096]{1,0:T(8,128)(2,1)}, u32[]{:S(2)}) copy-start(bf16[32,4096]{1,0:T(8,128)(2,1)} %spectra.1.own.refs_0_) | copy-start | bytes 786436
  22.5 11.8 %collective-permute-start.1 = (bf16[32,4096]{1,0:T(8,128)(2,1)S(1)}, bf16[32,4096]{1,0:T(8,128)(2,1)S(1)}, u32[]{:S(2)}, u32[]{:S(2)}) collective-permute-start(bf16[32,4096]{1,0:T(8,128)(2,1)S(1)} %collective-permute-done.refs_1_), channel_id=1, source_target_pairs={{0,2},{1,3},{2,0},{3,1},{4,6},{5,7},{6,4},{7,5},{8,10},{9,11},{10,... | collective-permute-start | bytes 786440 | tf_op jit(solution)/shard_map/ppermute | solution.py:378
  24.1 11.3 %collective-permute-start.3 = (bf16[32,4096]{1,0:T(8,128)(2,1)S(1)}, bf16[32,4096]{1,0:T(8,128)(2,1)S(1)}, u32[]{:S(2)}, u32[]{:S(2)}) collective-permute-start(bf16[32,4096]{1,0:T(8,128)(2,1)S(1)} %broadcast_select_fusion), channel_id=1, source_target_pairs={{0,14},{1,15},{2,0},{3,1},{4,2},{5,3},{6,4},{7,5},{8,6},{9,7},{10,... | collective-permute-start | bytes 786440 | tf_op jit(solution)/shard_map/ppermute | solution.py:378
  28.3 10.0 %collective-permute-start.2 = (bf16[32,4096]{1,0:T(8,128)(2,1)S(1)}, bf16[32,4096]{1,0:T(8,128)(2,1)S(1)}, u32[]{:S(2)}, u32[]{:S(2)}) collective-permute-start(bf16[32,4096]{1,0:T(8,128)(2,1)S(1)} %collective-permute-done.refs_1_), channel_id=1, source_target_pairs={{0,12},{1,13},{2,14},{3,15},{4,0},{5,1},{6,2},{7,3},{8,4},{9,5},{1... | collective-permute-start | bytes 786440 | tf_op jit(solution)/shard_map/ppermute | solution.py:378
  34.3 4.0 %collective-permute-start.5 = (bf16[32,4096]{1,0:T(8,128)(2,1)S(1)}, bf16[32,4096]{1,0:T(8,128)(2,1)S(1)}, u32[]{:S(2)}, u32[]{:S(2)}) collective-permute-start(bf16[32,4096]{1,0:T(8,128)(2,1)S(1)} %copy-done.1), channel_id=1, source_target_pairs={{0,1},{1,0},{2,3},{3,2},{4,5},{5,4},{6,7},{7,6},{8,9},{9,8},{10,11... | collective-permute-start | bytes 786440 | tf_op jit(solution)/shard_map/ppermute | solution.py:378
  35.3 3.0 %collective-permute-start.4 = (bf16[32,4096]{1,0:T(8,128)(2,1)S(1)}, bf16[32,4096]{1,0:T(8,128)(2,1)S(1)}, u32[]{:S(2)}, u32[]{:S(2)}) collective-permute-start(bf16[32,4096]{1,0:T(8,128)(2,1)S(1)} %collective-permute-done.3.refs_7_), channel_id=1, source_target_pairs={{0,1},{1,0},{2,3},{3,2},{4,5},{5,4},{6,7},{7,6},{8,9},{9,8},{10,11... | collective-permute-start | bytes 786440 | tf_op jit(solution)/shard_map/ppermute | solution.py:378
  35.3 3.0 %collective-permute-start.6 = (bf16[32,4096]{1,0:T(8,128)(2,1)S(1)}, bf16[32,4096]{1,0:T(8,128)(2,1)S(1)}, u32[]{:S(2)}, u32[]{:S(2)}) collective-permute-start(bf16[32,4096]{1,0:T(8,128)(2,1)S(1)} %collective-permute-done.refs_1_), channel_id=1, source_target_pairs={{0,1},{1,0},{2,3},{3,2},{4,5},{5,4},{6,7},{7,6},{8,9},{9,8},{10,11... | collective-permute-start | bytes 786440 | tf_op jit(solution)/shard_map/ppermute | solution.py:378
  35.8 2.5 %collective-permute-start.8 = (bf16[32,4096]{1,0:T(8,128)(2,1)S(1)}, bf16[32,4096]{1,0:T(8,128)(2,1)S(1)}, u32[]{:S(2)}, u32[]{:S(2)}) collective-permute-start(bf16[32,4096]{1,0:T(8,128)(2,1)S(1)} %collective-permute-done.1.refs_5_), channel_id=1, source_target_pairs={{0,1},{1,0},{2,3},{3,2},{4,5},{5,4},{6,7},{7,6},{8,9},{9,8},{10,11... | collective-permute-start | bytes 786440 | tf_op jit(solution)/shard_map/ppermute | solution.py:378
  38.3 1.6 %collective-permute-start.7 = (bf16[32,4096]{1,0:T(8,128)(2,1)S(1)}, bf16[32,4096]{1,0:T(8,128)(2,1)S(1)}, u32[]{:S(2)}, u32[]{:S(2)}) collective-permute-start(bf16[32,4096]{1,0:T(8,128)(2,1)S(1)} %collective-permute-done.2.refs_3_), channel_id=1, source_target_pairs={{0,1},{1,0},{2,3},{3,2},{4,5},{5,4},{6,7},{7,6},{8,9},{9,8},{10,11... | collective-permute-start | bytes 786440 | tf_op jit(solution)/shard_map/ppermute | solution.py:378
where the time goes:
time: 43.8 us; the launch traced here: 43.5 us
  Pallas kernels  21.2 us (48%)
  starting transfers between devices  11.5 us (26%)
  waiting for transfers between devices  9.77 us (22%)
  local copies, waits for them, and re-layouts  0.99 us (2%)
    pallas_call x1, Pallas kernels, local(): pl.pallas_call(functools.partial(spectra_kernel, halves, own, halo), name...  11.5 us
    ppermute x9, starting transfers between devices, exchange(): return lax.ppermute(value, 'chan', pairs)  11.5 us
    ppermute x9, waiting for transfers between devices, exchange(): return lax.ppermute(value, 'chan', pairs)  9.77 us
    pallas_call x2, Pallas kernels, product(): pl.pallas_call(functools.partial(product_kernel, late, chan_count, norm_s...  6.03 us
    pallas_call x1, Pallas kernels, local(): pl.pallas_call(functools.partial(rotate_kernel, lags), name='rotate', gri...  3.66 us
    unnamed x8, local copies, waits for them, and re-layouts  0.99 us
  transfers between devices with their start and end apart: 9, of which 5 were waited for; matrix products, arithmetic and copies ran while one was open for 0% of the time, Pallas kernels for 14%

commit v1 on v0

--- a/solution.py
+++ b/solution.py
@@ -477,7 +477,18 @@
 
     every = range(chan_count)
     down = [(i, (i - 4) % chan_count) for i in every]
-    down_2 = [(i, (i - 2) % chan_count) for i in every]
+    top = chan_count - 4
+
+    def far_target(i):
+        return i if i >= top else (i - 4 if i >= 4 else top - 4 + i)
+
+    def other_target(i):
+        if i & 2:
+            return i - 2
+        return i + 2 if i >= top else (i - 2 if i >= 4 else top - 2 + i)
+
+    far_pairs = [(i, far_target(i)) for i in every]
+    other_pairs = [(i, other_target(i)) for i in every]
     across = [(i, i ^ 2) for i in every]
     cores = [(i, i ^ 1) for i in every]
     side = lax.rem(lax.axis_index("chan") // 2, 2)
@@ -485,8 +496,8 @@
     ahead = exchange(spectra, down)
     ahead, rotated = lax.optimization_barrier((ahead, rotated))
     cross = exchange(ahead, across)
-    other = exchange(jnp.where(side == 0, ahead, spectra), down_2)
-    far = exchange(ahead, down)
+    other = exchange(jnp.where(side == 0, ahead, spectra), other_pairs)
+    far = exchange(ahead, far_pairs)
     early = product((spectra, ahead), None)
     kept, ahead, cross, early = lax.optimization_barrier((spectra, ahead, cross, early))
     own_swapped = exchange(kept, cores)

time: 43.8 us -> 42.7 us (0.975)
  waiting for transfers between devices: 9.77 us -> 9.14 us
  starting transfers between devices: 11.5 us -> 11 us
    ppermute x9, waiting for transfers between devices: 9.77 us -> 9.14 us  [exchange(): return lax.ppermute(value, 'chan', pairs)]
    ppermute x9, starting transfers between devices: 11.5 us -> 11 us  [exchange(): return lax.ppermute(value, 'chan', pairs)]
  transfers between devices with their start and end apart: 9 -> 9, of which waited for: 5 -> 8; matrix products, arithmetic and copies ran while one was open for 0% -> 0% of each run, Pallas kernels for 14% -> 14%
where the time goes in v1:
time: 42.7 us; the launch traced here: 42.4 us
  Pallas kernels  21.2 us (50%)
  starting transfers between devices  11 us (26%)
  waiting for transfers between devices  9.14 us (21%)
  local copies, waits for them, and re-layouts  0.99 us (2%)
    pallas_call x1, Pallas kernels, local(): pl.pallas_call(functools.partial(spectra_kernel, halves, own, halo), name...  11.5 us
    ppermute x9, starting transfers between devices, exchange(): return lax.ppermute(value, 'chan', pairs)  11 us
    ppermute x9, waiting for transfers between devices, exchange(): return lax.ppermute(value, 'chan', pairs)  9.14 us
    pallas_call x2, Pallas kernels, product(): pl.pallas_call(functools.partial(product_kernel, late, chan_count, norm_s...  6.03 us
    pallas_call x1, Pallas kernels, local(): pl.pallas_call(functools.partial(rotate_kernel, lags), name='rotate', gri...  3.66 us
    unnamed x8, local copies, waits for them, and re-layouts  0.99 us
  transfers between devices with their start and end apart: 9, of which 8 were waited for; matrix products, arithmetic and copies ran while one was open for 0% of the time, Pallas kernels for 14%

profile of v1, /device:TPU:0, one launch (start us, length us, event | category | flops | bytes accessed | tf_op | source)
XLA Modules:
  0.0 42.4 jit_solution(12883916713216752713)
XLA Ops:
  0.0 0.0 copy-start.2
  0.0 0.0 copy-start.3
  0.0 11.5 %spectra.1.own.refs_0_ = bf16[32,4096]{1,0:T(8,128)(2,1)} custom-call(s32[32]{0:T(128)} %dead.1, s32[8]{0:T(128)} %offs, f32[32,32768]{1,0:T(8,128)} %x_hbm.1, bf16[512,1152]{1,0:T(8,128)(2,1)} %constant.30.clone.table_hbm), custom_call_target="tpu_custom_call" | custom-call | flops 7000000000 | bytes 8388608 | tf_op jit(solution)/shard_map/spectra/pallas_call | solution.py:410
  11.6 5.1 %collective-permute-start = (bf16[32,4096]{1,0:T(8,128)(2,1)}, bf16[32,4096]{1,0:T(8,128)(2,1)S(1)}, u32[]{:S(2)}, u32[]{:S(2)}) collective-permute-start(bf16[32,4096]{1,0:T(8,128)(2,1)} %spectra.1.own.refs_0_), channel_id=1, source_target_pairs={{0,12},{1,13},{2,14},{3,15},{4,0},{5,1},{6,2},{7,3},{8,4},{9,5},{1... | collective-permute-start | bytes 786440 | tf_op jit(solution)/shard_map/ppermute | solution.py:378
  16.7 0.0 copy-done.2
  16.7 0.0 copy-done.3
  16.7 0.0 copy-start
  16.7 1.0 %copy-done = bf16[32,4096]{1,0:T(8,128)(2,1)S(1)} copy-done((bf16[32,4096]{1,0:T(8,128)(2,1)S(1)}, bf16[32,4096]{1,0:T(8,128)(2,1)}, u32[]{:S(2)}) %copy-start) | copy-done | bytes 262168
  17.6 0.0 copy-start.1
  17.6 3.7 %rotate.1.rotated = bf16[1024,4096]{1,0:T(8,128)(2,1)S(1)} custom-call(bf16[32,4096]{1,0:T(8,128)(2,1)S(1)} %copy-done, f32[32,256]{1,0:T(8,128)S(1)} %copy-done.3, f32[32,256]{1,0:T(8,128)S(1)} %copy-done.2), custom_call_target="tpu_custom_call" | custom-call | flops 4000000000 | bytes 8388608 | tf_op jit(solution)/shard_map/rotate/pallas_call | solution.py:441
  21.3 1.2 %collective-permute-done.refs_1_ = bf16[32,4096]{1,0:T(8,128)(2,1)S(1)} collective-permute-done((bf16[32,4096]{1,0:T(8,128)(2,1)}, bf16[32,4096]{1,0:T(8,128)(2,1)S(1)}, u32[]{:S(2)}, u32[]{:S(2)}) %collective-permute-start) | collective-permute-done | bytes 262176 | tf_op jit(solution)/shard_map/ppermute | solution.py:378
  22.5 1.5 %collective-permute-start.1 = (bf16[32,4096]{1,0:T(8,128)(2,1)S(1)}, bf16[32,4096]{1,0:T(8,128)(2,1)S(1)}, u32[]{:S(2)}, u32[]{:S(2)}) collective-permute-start(bf16[32,4096]{1,0:T(8,128)(2,1)S(1)} %collective-permute-done.refs_1_), channel_id=1, source_target_pairs={{0,2},{1,3},{2,0},{3,1},{4,6},{5,7},{6,4},{7,5},{8,10},{9,11},{10,... | collective-permute-start | bytes 786440 | tf_op jit(solution)/shard_map/ppermute | solution.py:378
  24.1 1.4 %collective-permute-start.3 = (bf16[32,4096]{1,0:T(8,128)(2,1)S(1)}, bf16[32,4096]{1,0:T(8,128)(2,1)S(1)}, u32[]{:S(2)}, u32[]{:S(2)}) collective-permute-start(bf16[32,4096]{1,0:T(8,128)(2,1)S(1)} %broadcast_select_fusion), channel_id=1, source_target_pairs={{0,10},{1,11},{2,0},{3,1},{4,2},{5,3},{6,4},{7,5},{8,6},{9,7},{10,... | collective-permute-start | bytes 786440 | tf_op jit(solution)/shard_map/ppermute | solution.py:378
  25.4 2.3 %collective-permute-start.2 = (bf16[32,4096]{1,0:T(8,128)(2,1)S(1)}, bf16[32,4096]{1,0:T(8,128)(2,1)S(1)}, u32[]{:S(2)}, u32[]{:S(2)}) collective-permute-start(bf16[32,4096]{1,0:T(8,128)(2,1)S(1)} %collective-permute-done.refs_1_), channel_id=1, source_target_pairs={{0,8},{1,9},{2,10},{3,11},{4,0},{5,1},{6,2},{7,3},{8,4},{9,5},{10,... | collective-permute-start | bytes 786440 | tf_op jit(solution)/shard_map/ppermute | solution.py:378
  27.8 0.0 copy-done.1
  27.8 2.4 %early_product.1.refs_0_ = f32[1024,256]{1,0:T(8,128)S(1)} custom-call(s32[1]{0:T(128)} %bitcast.place, bf16[1024,4096]{1,0:T(8,128)(2,1)S(1)} %rotate.1.rotated, bf16[32,4096]{1,0:T(8,128)(2,1)S(1)} %copy-done.1, bf16[32,4096]{1,0:T(8,128)(2,1)S(1)} %collective-permute-done.refs_1_), custom_call_target="tpu_custom_call" | custom-call | flops 2147483648 | bytes 6291456 | tf_op jit(solution)/shard_map/early_product/pallas_call | solution.py:461
  30.2 4.1 %collective-permute-done.1.refs_5_ = bf16[32,4096]{1,0:T(8,128)(2,1)S(1)} collective-permute-done((bf16[32,4096]{1,0:T(8,128)(2,1)S(1)}, bf16[32,4096]{1,0:T(8,128)(2,1)S(1)}, u32[]{:S(2)}, u32[]{:S(2)}) %collective-permute-start.1) | collective-permute-done | bytes 262176 | tf_op jit(solution)/shard_map/ppermute | solution.py:378
  34.3 0.0 collective-permute-start.5
  34.3 1.0 %collective-permute-done.3.refs_7_ = bf16[32,4096]{1,0:T(8,128)(2,1)S(1)} collective-permute-done((bf16[32,4096]{1,0:T(8,128)(2,1)S(1)}, bf16[32,4096]{1,0:T(8,128)(2,1)S(1)}, u32[]{:S(2)}, u32[]{:S(2)}) %collective-permute-start.3) | collective-permute-done | bytes 262176 | tf_op jit(solution)/shard_map/ppermute | solution.py:378
  35.3 0.0 collective-permute-start.4
  35.3 0.5 %collective-permute-start.6 = (bf16[32,4096]{1,0:T(8,128)(2,1)S(1)}, bf16[32,4096]{1,0:T(8,128)(2,1)S(1)}, u32[]{:S(2)}, u32[]{:S(2)}) collective-permute-start(bf16[32,4096]{1,0:T(8,128)(2,1)S(1)} %collective-permute-done.refs_1_), channel_id=1, source_target_pairs={{0,1},{1,0},{2,3},{3,2},{4,5},{5,4},{6,7},{7,6},{8,9},{9,8},{10,11... | collective-permute-start | bytes 786440 | tf_op jit(solution)/shard_map/ppermute | solution.py:378
  35.8 0.0 collective-permute-start.8
  35.8 0.8 %collective-permute-done.2.refs_3_ = bf16[32,4096]{1,0:T(8,128)(2,1)S(1)} collective-permute-done((bf16[32,4096]{1,0:T(8,128)(2,1)S(1)}, bf16[32,4096]{1,0:T(8,128)(2,1)S(1)}, u32[]{:S(2)}, u32[]{:S(2)}) %collective-permute-start.2) | collective-permute-done | bytes 262176 | tf_op jit(solution)/shard_map/ppermute | solution.py:378
  36.6 0.2 collective-permute-done.4.refs_8_
  36.9 0.0 collective-permute-done.5.refs_1_
  36.9 0.4 collective-permute-done.6.refs_2_
  37.2 0.1 collective-permute-start.7
  37.4 0.2 collective-permute-done.8.refs_6_
  37.6 1.2 %collective-permute-done.7.refs_4_ = bf16[32,4096]{1,0:T(8,128)(2,1)S(1)} collective-permute-done((bf16[32,4096]{1,0:T(8,128)(2,1)S(1)}, bf16[32,4096]{1,0:T(8,128)(2,1)S(1)}, u32[]{:S(2)}, u32[]{:S(2)}) %collective-permute-start.7) | collective-permute-done | bytes 262176 | tf_op jit(solution)/shard_map/ppermute | solution.py:378
  38.8 3.6 %late_product.1 = bf16[1024,256]{1,0:T(8,128)(2,1)} custom-call(s32[1]{0:T(128)} %bitcast.place, bf16[1024,4096]{1,0:T(8,128)(2,1)S(1)} %rotate.1.rotated, f32[1024,256]{1,0:T(8,128)S(1)} %early_product.1.refs_0_, bf16[32,4096]{1,0:T(8,128)(2,1)S(1)} %collective-permute-done.5.refs_1_, bf16[32,4096]{1,0:T(8,128)(2,1)S(1)} %collective-permute-done.6.refs_2_, ...), custom_call_target="tpu_custom_call" | custom-call | flops 2147483648 | bytes 6291456 | tf_op jit(solution)/shard_map/late_product/pallas_call | solution.py:461
  (1 shorter events, 0.0 us)
Async XLA Ops:
  0.0 16.7 %copy-start.2 = (f32[32,256]{1,0:T(8,128)S(1)}, f32[32,256]{1,0:T(8,128)}, u32[]{:S(2)}) copy-start(f32[32,256]{1,0:T(8,128)} %constant.32.clone.sin_lag) | copy-start | bytes 98308
  0.0 16.7 %copy-start.3 = (f32[32,256]{1,0:T(8,128)S(1)}, f32[32,256]{1,0:T(8,128)}, u32[]{:S(2)}) copy-start(f32[32,256]{1,0:T(8,128)} %constant.31.clone.cos_lag) | copy-start | bytes 98308
  11.6 11.0 %collective-permute-start = (bf16[32,4096]{1,0:T(8,128)(2,1)}, bf16[32,4096]{1,0:T(8,128)(2,1)S(1)}, u32[]{:S(2)}, u32[]{:S(2)}) collective-permute-start(bf16[32,4096]{1,0:T(8,128)(2,1)} %spectra.1.own.refs_0_), channel_id=1, source_target_pairs={{0,12},{1,13},{2,14},{3,15},{4,0},{5,1},{6,2},{7,3},{8,4},{9,5},{1... | collective-permute-start | bytes 786440 | tf_op jit(solution)/shard_map/ppermute | solution.py:378
  16.7 1.0 %copy-start = (bf16[32,4096]{1,0:T(8,128)(2,1)S(1)}, bf16[32,4096]{1,0:T(8,128)(2,1)}, u32[]{:S(2)}) copy-start(bf16[32,4096]{1,0:T(8,128)(2,1)} %spectra.1.own.refs_0_) | copy-start | bytes 786436
  17.6 10.2 %copy-start.1 = (bf16[32,4096]{1,0:T(8,128)(2,1)S(1)}, bf16[32,4096]{1,0:T(8,128)(2,1)}, u32[]{:S(2)}) copy-start(bf16[32,4096]{1,0:T(8,128)(2,1)} %spectra.1.own.refs_0_) | copy-start | bytes 786436
  22.5 11.8 %collective-permute-start.1 = (bf16[32,4096]{1,0:T(8,128)(2,1)S(1)}, bf16[32,4096]{1,0:T(8,128)(2,1)S(1)}, u32[]{:S(2)}, u32[]{:S(2)}) collective-permute-start(bf16[32,4096]{1,0:T(8,128)(2,1)S(1)} %collective-permute-done.refs_1_), channel_id=1, source_target_pairs={{0,2},{1,3},{2,0},{3,1},{4,6},{5,7},{6,4},{7,5},{8,10},{9,11},{10,... | collective-permute-start | bytes 786440 | tf_op jit(solution)/shard_map/ppermute | solution.py:378
  24.1 11.3 %collective-permute-start.3 = (bf16[32,4096]{1,0:T(8,128)(2,1)S(1)}, bf16[32,4096]{1,0:T(8,128)(2,1)S(1)}, u32[]{:S(2)}, u32[]{:S(2)}) collective-permute-start(bf16[32,4096]{1,0:T(8,128)(2,1)S(1)} %broadcast_select_fusion), channel_id=1, source_target_pairs={{0,10},{1,11},{2,0},{3,1},{4,2},{5,3},{6,4},{7,5},{8,6},{9,7},{10,... | collective-permute-start | bytes 786440 | tf_op jit(solution)/shard_map/ppermute | solution.py:378
  25.4 11.2 %collective-permute-start.2 = (bf16[32,4096]{1,0:T(8,128)(2,1)S(1)}, bf16[32,4096]{1,0:T(8,128)(2,1)S(1)}, u32[]{:S(2)}, u32[]{:S(2)}) collective-permute-start(bf16[32,4096]{1,0:T(8,128)(2,1)S(1)} %collective-permute-done.refs_1_), channel_id=1, source_target_pairs={{0,8},{1,9},{2,10},{3,11},{4,0},{5,1},{6,2},{7,3},{8,4},{9,5},{10,... | collective-permute-start | bytes 786440 | tf_op jit(solution)/shard_map/ppermute | solution.py:378
  34.3 2.5 %collective-permute-start.5 = (bf16[32,4096]{1,0:T(8,128)(2,1)S(1)}, bf16[32,4096]{1,0:T(8,128)(2,1)S(1)}, u32[]{:S(2)}, u32[]{:S(2)}) collective-permute-start(bf16[32,4096]{1,0:T(8,128)(2,1)S(1)} %copy-done.1), channel_id=1, source_target_pairs={{0,1},{1,0},{2,3},{3,2},{4,5},{5,4},{6,7},{7,6},{8,9},{9,8},{10,11... | collective-permute-start | bytes 786440 | tf_op jit(solution)/shard_map/ppermute | solution.py:378
  35.3 1.5 %collective-permute-start.4 = (bf16[32,4096]{1,0:T(8,128)(2,1)S(1)}, bf16[32,4096]{1,0:T(8,128)(2,1)S(1)}, u32[]{:S(2)}, u32[]{:S(2)}) collective-permute-start(bf16[32,4096]{1,0:T(8,128)(2,1)S(1)} %collective-permute-done.3.refs_7_), channel_id=1, source_target_pairs={{0,1},{1,0},{2,3},{3,2},{4,5},{5,4},{6,7},{7,6},{8,9},{9,8},{10,11... | collective-permute-start | bytes 786440 | tf_op jit(solution)/shard_map/ppermute | solution.py:378
  35.3 1.9 %collective-permute-start.6 = (bf16[32,4096]{1,0:T(8,128)(2,1)S(1)}, bf16[32,4096]{1,0:T(8,128)(2,1)S(1)}, u32[]{:S(2)}, u32[]{:S(2)}) collective-permute-start(bf16[32,4096]{1,0:T(8,128)(2,1)S(1)} %collective-permute-done.refs_1_), channel_id=1, source_target_pairs={{0,1},{1,0},{2,3},{3,2},{4,5},{5,4},{6,7},{7,6},{8,9},{9,8},{10,11... | collective-permute-start | bytes 786440 | tf_op jit(solution)/shard_map/ppermute | solution.py:378
  35.8 1.8 %collective-permute-start.8 = (bf16[32,4096]{1,0:T(8,128)(2,1)S(1)}, bf16[32,4096]{1,0:T(8,128)(2,1)S(1)}, u32[]{:S(2)}, u32[]{:S(2)}) collective-permute-start(bf16[32,4096]{1,0:T(8,128)(2,1)S(1)} %collective-permute-done.1.refs_5_), channel_id=1, source_target_pairs={{0,1},{1,0},{2,3},{3,2},{4,5},{5,4},{6,7},{7,6},{8,9},{9,8},{10,11... | collective-permute-start | bytes 786440 | tf_op jit(solution)/shard_map/ppermute | solution.py:378
  37.2 1.5 %collective-permute-start.7 = (bf16[32,4096]{1,0:T(8,128)(2,1)S(1)}, bf16[32,4096]{1,0:T(8,128)(2,1)S(1)}, u32[]{:S(2)}, u32[]{:S(2)}) collective-permute-start(bf16[32,4096]{1,0:T(8,128)(2,1)S(1)} %collective-permute-done.2.refs_3_), channel_id=1, source_target_pairs={{0,1},{1,0},{2,3},{3,2},{4,5},{5,4},{6,7},{7,6},{8,9},{9,8},{10,11... | collective-permute-start | bytes 786440 | tf_op jit(solution)/shard_map/ppermute | solution.py:378

commit v2 on v1

--- a/solution.py
+++ b/solution.py
@@ -82,30 +82,33 @@
     bulk = min(own + 1, halves)
     edges = min(own + 2, halves)
     width = halves * HOP
-    middle = HOP // 2 + H
-    firsts, seconds = [], []
-    for j in range(halves):
-        firsts.append((j * HOP - (H if j or halo else 0), j * HOP + middle))
-        seconds.append((j * HOP + middle, (j + 1) * HOP - H if j + 1 < halves else width + halo))
+    cuts = [HOP // 4 + H, HOP // 2 + H]
+    pieces = []
+    for part in range(3):
+        for j in range(halves):
+            begin = j * HOP + cuts[part - 1] if part else j * HOP - (H if j or halo else 0)
+            end = (j + 1) * HOP - H if j + 1 < halves else width + halo
+            pieces.append((begin, j * HOP + cuts[part] if part < 2 else end))
     copies = [
         pltpu.make_async_copy(
             x_hbm.at[:, pl.ds(halo + begin, end - begin)], x.at[:, pl.ds(H + begin, end - begin)],
             sems.at[i],
         )
-        for i, (begin, end) in enumerate(firsts + seconds)
+        for i, (begin, end) in enumerate(pieces)
     ]
-    table_copy = pltpu.make_async_copy(table_hbm, table, sems.at[2 * halves])
-    for copy in copies[:halves] + [table_copy] + copies[halves:]:
+    table_copy = pltpu.make_async_copy(table_hbm, table, sems.at[3 * halves])
+    for copy in copies[:2 * halves] + [table_copy] + copies[2 * halves:]:
         copy.start()
     if not halo:
         for begin in (0, H + width):
             absolute[:, begin:begin + H] = jnp.zeros((channels, H), BF16)
 
-    def arrive(ids):
+    def arrive(part):
+        ids = range(part * halves, (part + 1) * halves)
         for i in ids:
             copies[i].wait()
         for i in ids:
-            begin, end = (firsts + seconds)[i]
+            begin, end = pieces[i]
             here = slice(H + begin, H + end)
             absolute[:, here] = jnp.abs(x[:, here]).astype(BF16)
 
@@ -186,14 +189,15 @@
     begins = {}
     place = 0
     waiting = None
-    arrive(range(halves))
-    table_copy.wait()
     for g in range(0, groups, 2):
-        if g == groups // 2:
-            arrive(range(halves, 2 * halves))
+        if g < 4:
+            arrive(g // 2)
         start = place
         found, place = normalise([g, g + 1], place)
         begins.update(found)
+        if g == 2:
+            arrive(2)
+            table_copy.wait()
         if waiting:
             transform(*waiting)
         waiting = (start, place)
@@ -420,7 +424,7 @@
             pltpu.VMEM((part_rows, GROUP), BF16),
             pltpu.VMEM((part_rows, 2 * NF + 128), F32),
             pltpu.VMEM(table.shape, BF16),
-            pltpu.SemaphoreType.DMA((2 * halves + 1,)),
+            pltpu.SemaphoreType.DMA((3 * halves + 1,)),
         ],
         compiler_params=pltpu.CompilerParams(vmem_limit_bytes=60 * 1024 * 1024),
         cost_estimate=pl.CostEstimate(
@@ -499,15 +503,14 @@
     other = exchange(jnp.where(side == 0, ahead, spectra), other_pairs)
     far = exchange(ahead, far_pairs)
     early = product((spectra, ahead), None)
-    kept, ahead, cross, early = lax.optimization_barrier((spectra, ahead, cross, early))
+    kept, ahead, other, early = lax.optimization_barrier((spectra, ahead, other, early))
     own_swapped = exchange(kept, cores)
     ahead_swapped = exchange(ahead, cores)
-    other_swapped = exchange(other, cores)
-    far, other_swapped, own_swapped, ahead_swapped = lax.optimization_barrier(
-        (far, other_swapped, own_swapped, ahead_swapped)
+    cross, own_swapped, ahead_swapped = lax.optimization_barrier(
+        (cross, own_swapped, ahead_swapped)
     )
     blocks = (own_swapped, ahead_swapped, far, exchange(far, cores), cross,
-              exchange(cross, cores), other, other_swapped)
+              exchange(cross, cores), other, exchange(other, cores))
     return product(blocks, early).reshape(lags, channels, NPART)
 
 

time: 42.7 us -> 41.7 us (0.977)
  waiting for transfers between devices: 9.14 us -> 8.01 us
  starting transfers between devices: 11 us -> 11.6 us
    ppermute x9, waiting for transfers between devices: 9.14 us -> 8.01 us  [exchange(): return lax.ppermute(value, 'chan', pairs)]
    ppermute x9, starting transfers between devices: 11 us -> 11.6 us  [exchange(): return lax.ppermute(value, 'chan', pairs)]
    pallas_call x1, Pallas kernels: 11.5 us -> 11.1 us  [local(): pl.pallas_call(functools.partial(spectra_kernel, halves, own, halo), name...]
  transfers between devices with their start and end apart: 9 -> 9, of which waited for: 8 -> 5; matrix products, arithmetic and copies ran while one was open for 0% -> 0% of each run, Pallas kernels for 14% -> 15%
where the time goes in v2:
time: 41.7 us; the launch traced here: 41.4 us
  Pallas kernels  20.8 us (50%)
  starting transfers between devices  11.6 us (28%)
  waiting for transfers between devices  8.01 us (19%)
  local copies, waits for them, and re-layouts  0.99 us (2%)
    ppermute x9, starting transfers between devices, exchange(): return lax.ppermute(value, 'chan', pairs)  11.6 us
    pallas_call x1, Pallas kernels, local(): pl.pallas_call(functools.partial(spectra_kernel, halves, own, halo), name...  11.1 us
    ppermute x9, waiting for transfers between devices, exchange(): return lax.ppermute(value, 'chan', pairs)  8.01 us
    pallas_call x2, Pallas kernels, product(): pl.pallas_call(functools.partial(product_kernel, late, chan_count, norm_s...  6.03 us
    pallas_call x1, Pallas kernels, local(): pl.pallas_call(functools.partial(rotate_kernel, lags), name='rotate', gri...  3.66 us
    unnamed x8, local copies, waits for them, and re-layouts  0.99 us
  transfers between devices with their start and end apart: 9, of which 5 were waited for; matrix products, arithmetic and copies ran while one was open for 0% of the time, Pallas kernels for 15%

profile of v2, /device:TPU:0, one launch (start us, length us, event | category | flops | bytes accessed | tf_op | source)
XLA Modules:
  0.0 41.4 jit_solution(17061349503628942443)
XLA Ops:
  0.0 0.0 copy-start.2
  0.0 0.0 copy-start.3
  0.0 11.1 %spectra.1.own.refs_0_ = bf16[32,4096]{1,0:T(8,128)(2,1)} custom-call(s32[32]{0:T(128)} %dead.1, s32[8]{0:T(128)} %offs, f32[32,32768]{1,0:T(8,128)} %x_hbm.1, bf16[512,1152]{1,0:T(8,128)(2,1)} %constant.30.clone.table_hbm), custom_call_target="tpu_custom_call" | custom-call | flops 7000000000 | bytes 8388608 | tf_op jit(solution)/shard_map/spectra/pallas_call | solution.py:414
  11.1 5.1 %collective-permute-start = (bf16[32,4096]{1,0:T(8,128)(2,1)}, bf16[32,4096]{1,0:T(8,128)(2,1)S(1)}, u32[]{:S(2)}, u32[]{:S(2)}) collective-permute-start(bf16[32,4096]{1,0:T(8,128)(2,1)} %spectra.1.own.refs_0_), channel_id=1, source_target_pairs={{0,12},{1,13},{2,14},{3,15},{4,0},{5,1},{6,2},{7,3},{8,4},{9,5},{1... | collective-permute-start | bytes 786440 | tf_op jit(solution)/shard_map/ppermute | solution.py:382
  16.2 0.0 copy-done.2
  16.2 0.0 copy-done.3
  16.2 0.0 copy-start
  16.2 1.0 %copy-done = bf16[32,4096]{1,0:T(8,128)(2,1)S(1)} copy-done((bf16[32,4096]{1,0:T(8,128)(2,1)S(1)}, bf16[32,4096]{1,0:T(8,128)(2,1)}, u32[]{:S(2)}) %copy-start) | copy-done | bytes 262168
  17.2 0.0 copy-start.1
  17.2 3.7 %rotate.1.rotated = bf16[1024,4096]{1,0:T(8,128)(2,1)S(1)} custom-call(bf16[32,4096]{1,0:T(8,128)(2,1)S(1)} %copy-done, f32[32,256]{1,0:T(8,128)S(1)} %copy-done.3, f32[32,256]{1,0:T(8,128)S(1)} %copy-done.2), custom_call_target="tpu_custom_call" | custom-call | flops 4000000000 | bytes 8388608 | tf_op jit(solution)/shard_map/rotate/pallas_call | solution.py:445
  20.9 1.2 %collective-permute-done.refs_1_ = bf16[32,4096]{1,0:T(8,128)(2,1)S(1)} collective-permute-done((bf16[32,4096]{1,0:T(8,128)(2,1)}, bf16[32,4096]{1,0:T(8,128)(2,1)S(1)}, u32[]{:S(2)}, u32[]{:S(2)}) %collective-permute-start) | collective-permute-done | bytes 262176 | tf_op jit(solution)/shard_map/ppermute | solution.py:382
  22.1 2.3 %collective-permute-start.1 = (bf16[32,4096]{1,0:T(8,128)(2,1)S(1)}, bf16[32,4096]{1,0:T(8,128)(2,1)S(1)}, u32[]{:S(2)}, u32[]{:S(2)}) collective-permute-start(bf16[32,4096]{1,0:T(8,128)(2,1)S(1)} %broadcast_select_fusion), channel_id=1, source_target_pairs={{0,10},{1,11},{2,0},{3,1},{4,2},{5,3},{6,4},{7,5},{8,6},{9,7},{10,... | collective-permute-start | bytes 786440 | tf_op jit(solution)/shard_map/ppermute | solution.py:382
  24.5 2.4 %collective-permute-start.5 = (bf16[32,4096]{1,0:T(8,128)(2,1)S(1)}, bf16[32,4096]{1,0:T(8,128)(2,1)S(1)}, u32[]{:S(2)}, u32[]{:S(2)}) collective-permute-start(bf16[32,4096]{1,0:T(8,128)(2,1)S(1)} %collective-permute-done.refs_1_), channel_id=1, source_target_pairs={{0,8},{1,9},{2,10},{3,11},{4,0},{5,1},{6,2},{7,3},{8,4},{9,5},{10,... | collective-permute-start | bytes 786440 | tf_op jit(solution)/shard_map/ppermute | solution.py:382
  26.8 0.7 %collective-permute-start.2 = (bf16[32,4096]{1,0:T(8,128)(2,1)S(1)}, bf16[32,4096]{1,0:T(8,128)(2,1)S(1)}, u32[]{:S(2)}, u32[]{:S(2)}) collective-permute-start(bf16[32,4096]{1,0:T(8,128)(2,1)S(1)} %collective-permute-done.refs_1_), channel_id=1, source_target_pairs={{0,2},{1,3},{2,0},{3,1},{4,6},{5,7},{6,4},{7,5},{8,10},{9,11},{10,... | collective-permute-start | bytes 786440 | tf_op jit(solution)/shard_map/ppermute | solution.py:382
  27.5 0.0 copy-done.1
  27.5 2.4 %early_product.1.refs_0_ = f32[1024,256]{1,0:T(8,128)S(1)} custom-call(s32[1]{0:T(128)} %bitcast.place, bf16[1024,4096]{1,0:T(8,128)(2,1)S(1)} %rotate.1.rotated, bf16[32,4096]{1,0:T(8,128)(2,1)S(1)} %copy-done.1, bf16[32,4096]{1,0:T(8,128)(2,1)S(1)} %collective-permute-done.refs_1_), custom_call_target="tpu_custom_call" | custom-call | flops 2147483648 | bytes 6291456 | tf_op jit(solution)/shard_map/early_product/pallas_call | solution.py:465
  29.9 1.3 %collective-permute-done.1.refs_7_ = bf16[32,4096]{1,0:T(8,128)(2,1)S(1)} collective-permute-done((bf16[32,4096]{1,0:T(8,128)(2,1)S(1)}, bf16[32,4096]{1,0:T(8,128)(2,1)S(1)}, u32[]{:S(2)}, u32[]{:S(2)}) %collective-permute-start.1) | collective-permute-done | bytes 262176 | tf_op jit(solution)/shard_map/ppermute | solution.py:382
  31.2 0.0 collective-permute-start.3
  31.2 0.5 %collective-permute-start.4 = (bf16[32,4096]{1,0:T(8,128)(2,1)S(1)}, bf16[32,4096]{1,0:T(8,128)(2,1)S(1)}, u32[]{:S(2)}, u32[]{:S(2)}) collective-permute-start(bf16[32,4096]{1,0:T(8,128)(2,1)S(1)} %collective-permute-done.refs_1_), channel_id=1, source_target_pairs={{0,1},{1,0},{2,3},{3,2},{4,5},{5,4},{6,7},{7,6},{8,9},{9,8},{10,11... | collective-permute-start | bytes 786440 | tf_op jit(solution)/shard_map/ppermute | solution.py:382
  31.7 0.0 collective-permute-start.8
  31.7 4.1 %collective-permute-done.5.refs_3_ = bf16[32,4096]{1,0:T(8,128)(2,1)S(1)} collective-permute-done((bf16[32,4096]{1,0:T(8,128)(2,1)S(1)}, bf16[32,4096]{1,0:T(8,128)(2,1)S(1)}, u32[]{:S(2)}, u32[]{:S(2)}) %collective-permute-start.5) | collective-permute-done | bytes 262176 | tf_op jit(solution)/shard_map/ppermute | solution.py:382
  35.9 0.0 collective-permute-start.6
  35.9 0.0 collective-permute-done.2.refs_5_
  35.9 0.0 collective-permute-done.3.refs_1_
  35.9 0.0 collective-permute-done.4.refs_2_
  35.9 0.6 %collective-permute-start.7 = (bf16[32,4096]{1,0:T(8,128)(2,1)S(1)}, bf16[32,4096]{1,0:T(8,128)(2,1)S(1)}, u32[]{:S(2)}, u32[]{:S(2)}) collective-permute-start(bf16[32,4096]{1,0:T(8,128)(2,1)S(1)} %collective-permute-done.2.refs_5_), channel_id=1, source_target_pairs={{0,1},{1,0},{2,3},{3,2},{4,5},{5,4},{6,7},{7,6},{8,9},{9,8},{10,11... | collective-permute-start | bytes 786440 | tf_op jit(solution)/shard_map/ppermute | solution.py:382
  36.5 0.9 %collective-permute-done.6.refs_4_ = bf16[32,4096]{1,0:T(8,128)(2,1)S(1)} collective-permute-done((bf16[32,4096]{1,0:T(8,128)(2,1)S(1)}, bf16[32,4096]{1,0:T(8,128)(2,1)S(1)}, u32[]{:S(2)}, u32[]{:S(2)}) %collective-permute-start.6) | collective-permute-done | bytes 262176 | tf_op jit(solution)/shard_map/ppermute | solution.py:382
  37.4 0.0 collective-permute-done.8.refs_8_
  37.4 0.4 collective-permute-done.7.refs_6_
  37.8 3.6 %late_product.1 = bf16[1024,256]{1,0:T(8,128)(2,1)} custom-call(s32[1]{0:T(128)} %bitcast.place, bf16[1024,4096]{1,0:T(8,128)(2,1)S(1)} %rotate.1.rotated, f32[1024,256]{1,0:T(8,128)S(1)} %early_product.1.refs_0_, bf16[32,4096]{1,0:T(8,128)(2,1)S(1)} %collective-permute-done.3.refs_1_, bf16[32,4096]{1,0:T(8,128)(2,1)S(1)} %collective-permute-done.4.refs_2_, ...), custom_call_target="tpu_custom_call" | custom-call | flops 2147483648 | bytes 6291456 | tf_op jit(solution)/shard_map/late_product/pallas_call | solution.py:465
  (1 shorter events, 0.0 us)
Async XLA Ops:
  0.0 16.2 %copy-start.2 = (f32[32,256]{1,0:T(8,128)S(1)}, f32[32,256]{1,0:T(8,128)}, u32[]{:S(2)}) copy-start(f32[32,256]{1,0:T(8,128)} %constant.32.clone.sin_lag) | copy-start | bytes 98308
  0.0 16.2 %copy-start.3 = (f32[32,256]{1,0:T(8,128)S(1)}, f32[32,256]{1,0:T(8,128)}, u32[]{:S(2)}) copy-start(f32[32,256]{1,0:T(8,128)} %constant.31.clone.cos_lag) | copy-start | bytes 98308
  11.1 11.0 %collective-permute-start = (bf16[32,4096]{1,0:T(8,128)(2,1)}, bf16[32,4096]{1,0:T(8,128)(2,1)S(1)}, u32[]{:S(2)}, u32[]{:S(2)}) collective-permute-start(bf16[32,4096]{1,0:T(8,128)(2,1)} %spectra.1.own.refs_0_), channel_id=1, source_target_pairs={{0,12},{1,13},{2,14},{3,15},{4,0},{5,1},{6,2},{7,3},{8,4},{9,5},{1... | collective-permute-start | bytes 786440 | tf_op jit(solution)/shard_map/ppermute | solution.py:382
  16.2 1.0 %copy-start = (bf16[32,4096]{1,0:T(8,128)(2,1)S(1)}, bf16[32,4096]{1,0:T(8,128)(2,1)}, u32[]{:S(2)}) copy-start(bf16[32,4096]{1,0:T(8,128)(2,1)} %spectra.1.own.refs_0_) | copy-start | bytes 786436
  17.2 10.3 %copy-start.1 = (bf16[32,4096]{1,0:T(8,128)(2,1)S(1)}, bf16[32,4096]{1,0:T(8,128)(2,1)}, u32[]{:S(2)}) copy-start(bf16[32,4096]{1,0:T(8,128)(2,1)} %spectra.1.own.refs_0_) | copy-start | bytes 786436
  22.1 9.1 %collective-permute-start.1 = (bf16[32,4096]{1,0:T(8,128)(2,1)S(1)}, bf16[32,4096]{1,0:T(8,128)(2,1)S(1)}, u32[]{:S(2)}, u32[]{:S(2)}) collective-permute-start(bf16[32,4096]{1,0:T(8,128)(2,1)S(1)} %broadcast_select_fusion), channel_id=1, source_target_pairs={{0,10},{1,11},{2,0},{3,1},{4,2},{5,3},{6,4},{7,5},{8,6},{9,7},{10,... | collective-permute-start | bytes 786440 | tf_op jit(solution)/shard_map/ppermute | solution.py:382
  24.5 11.4 %collective-permute-start.5 = (bf16[32,4096]{1,0:T(8,128)(2,1)S(1)}, bf16[32,4096]{1,0:T(8,128)(2,1)S(1)}, u32[]{:S(2)}, u32[]{:S(2)}) collective-permute-start(bf16[32,4096]{1,0:T(8,128)(2,1)S(1)} %collective-permute-done.refs_1_), channel_id=1, source_target_pairs={{0,8},{1,9},{2,10},{3,11},{4,0},{5,1},{6,2},{7,3},{8,4},{9,5},{10,... | collective-permute-start | bytes 786440 | tf_op jit(solution)/shard_map/ppermute | solution.py:382
  26.8 9.1 %collective-permute-start.2 = (bf16[32,4096]{1,0:T(8,128)(2,1)S(1)}, bf16[32,4096]{1,0:T(8,128)(2,1)S(1)}, u32[]{:S(2)}, u32[]{:S(2)}) collective-permute-start(bf16[32,4096]{1,0:T(8,128)(2,1)S(1)} %collective-permute-done.refs_1_), channel_id=1, source_target_pairs={{0,2},{1,3},{2,0},{3,1},{4,6},{5,7},{6,4},{7,5},{8,10},{9,11},{10,... | collective-permute-start | bytes 786440 | tf_op jit(solution)/shard_map/ppermute | solution.py:382
  31.2 4.7 %collective-permute-start.3 = (bf16[32,4096]{1,0:T(8,128)(2,1)S(1)}, bf16[32,4096]{1,0:T(8,128)(2,1)S(1)}, u32[]{:S(2)}, u32[]{:S(2)}) collective-permute-start(bf16[32,4096]{1,0:T(8,128)(2,1)S(1)} %copy-done.1), channel_id=1, source_target_pairs={{0,1},{1,0},{2,3},{3,2},{4,5},{5,4},{6,7},{7,6},{8,9},{9,8},{10,11... | collective-permute-start | bytes 786440 | tf_op jit(solution)/shard_map/ppermute | solution.py:382
  31.2 4.7 %collective-permute-start.4 = (bf16[32,4096]{1,0:T(8,128)(2,1)S(1)}, bf16[32,4096]{1,0:T(8,128)(2,1)S(1)}, u32[]{:S(2)}, u32[]{:S(2)}) collective-permute-start(bf16[32,4096]{1,0:T(8,128)(2,1)S(1)} %collective-permute-done.refs_1_), channel_id=1, source_target_pairs={{0,1},{1,0},{2,3},{3,2},{4,5},{5,4},{6,7},{7,6},{8,9},{9,8},{10,11... | collective-permute-start | bytes 786440 | tf_op jit(solution)/shard_map/ppermute | solution.py:382
  31.7 5.7 %collective-permute-start.8 = (bf16[32,4096]{1,0:T(8,128)(2,1)S(1)}, bf16[32,4096]{1,0:T(8,128)(2,1)S(1)}, u32[]{:S(2)}, u32[]{:S(2)}) collective-permute-start(bf16[32,4096]{1,0:T(8,128)(2,1)S(1)} %collective-permute-done.1.refs_7_), channel_id=1, source_target_pairs={{0,1},{1,0},{2,3},{3,2},{4,5},{5,4},{6,7},{7,6},{8,9},{9,8},{10,11... | collective-permute-start | bytes 786440 | tf_op jit(solution)/shard_map/ppermute | solution.py:382
  35.9 1.5 %collective-permute-start.6 = (bf16[32,4096]{1,0:T(8,128)(2,1)S(1)}, bf16[32,4096]{1,0:T(8,128)(2,1)S(1)}, u32[]{:S(2)}, u32[]{:S(2)}) collective-permute-start(bf16[32,4096]{1,0:T(8,128)(2,1)S(1)} %collective-permute-done.5.refs_3_), channel_id=1, source_target_pairs={{0,1},{1,0},{2,3},{3,2},{4,5},{5,4},{6,7},{7,6},{8,9},{9,8},{10,11... | collective-permute-start | bytes 786440 | tf_op jit(solution)/shard_map/ppermute | solution.py:382
  35.9 1.9 %collective-permute-start.7 = (bf16[32,4096]{1,0:T(8,128)(2,1)S(1)}, bf16[32,4096]{1,0:T(8,128)(2,1)S(1)}, u32[]{:S(2)}, u32[]{:S(2)}) collective-permute-start(bf16[32,4096]{1,0:T(8,128)(2,1)S(1)} %collective-permute-done.2.refs_5_), channel_id=1, source_target_pairs={{0,1},{1,0},{2,3},{3,2},{4,5},{5,4},{6,7},{7,6},{8,9},{9,8},{10,11... | collective-permute-start | bytes 786440 | tf_op jit(solution)/shard_map/ppermute | solution.py:382

commit v3 on v2

--- a/solution.py
+++ b/solution.py
@@ -75,7 +75,8 @@
 
 def spectra_kernel(
     halves, own, halo,
-    dead, offs, x_hbm, table_hbm, out, x, absolute, norm_high, norm_low, parts, table, sems,
+    dead, offs, x_hbm, table_hbm, out, x, absolute, norm_high, norm_low, parts,
+    same_sum, swap_sum, table, sems,
 ):
     channels = x.shape[0]
     groups = HOP // GROUP
@@ -201,18 +202,30 @@
         if waiting:
             transform(*waiting)
         waiting = (start, place)
-    transform(*waiting)
 
     def piece(name, j):
         return parts[begins[name] + j * channels:begins[name] + (j + 1) * channels, :]
 
+    def turned(j, ids):
+        same = swap = None
+        for g in ids:
+            value = piece(g, j)
+            first, second = value * turn_same[g:g + 1, :], value * turn_swap[g:g + 1, :]
+            same = first if same is None else same + first
+            swap = second if swap is None else swap + second
+        return same, swap
+
+    def rows_of(j):
+        return slice(j * channels, (j + 1) * channels)
+
+    for j in range(bulk):
+        same_sum[rows_of(j), :], swap_sum[rows_of(j), :] = turned(j, range(1, groups - 2))
+    transform(*waiting)
+
     def bulk_of(j):
-        same = jnp.zeros((channels, parts.shape[1]), F32)
-        swap = same
-        for g in range(1, groups):
-            value = piece(g, j)
-            same = same + value * turn_same[g:g + 1, :]
-            swap = swap + value * turn_swap[g:g + 1, :]
+        same, swap = turned(j, range(groups - 2, groups))
+        same = same + same_sum[rows_of(j), :]
+        swap = swap + swap_sum[rows_of(j), :]
         return same + jnp.concatenate(
             [swap[:, NF:2 * NF], swap[:, :NF], pltpu.roll(swap[:, 2 * NF:], 64, 1)], axis=1
         )
@@ -346,19 +359,15 @@
 def product_kernel(late, count, norm_scale, place, rotated, *refs):
     refs = list(refs)
     before = refs.pop(0) if late else None
-    out, partners, total = refs[-3:]
-    blocks = refs[:-3]
+    out, partners, turned, total = refs[-4:]
+    blocks = refs[:-4]
     channels = blocks[0].shape[0]
     (late_slots if late else early_slots)(place[0], count, channels, blocks, partners)
     rows, features = rotated.shape
     chunk = 2 * 2 * NF
     for begin in range(0, features, chunk):
-        turned = partners[:, begin:begin + chunk].T
-        product = dot(rotated[:, begin:begin + chunk], turned)
-        if begin == 0:
-            total[...] = product
-        else:
-            total[...] += product
+        turned[begin:begin + chunk, :] = partners[:, begin:begin + chunk].T
+    total[...] = dot(rotated[...], turned[...])
 
     row = lax.broadcasted_iota(jnp.int32, (channels, NPART), 0)
     column = lax.broadcasted_iota(jnp.int32, (channels, NPART), 1)
@@ -423,6 +432,8 @@
             pltpu.VMEM((part_rows, GROUP), BF16),
             pltpu.VMEM((part_rows, GROUP), BF16),
             pltpu.VMEM((part_rows, 2 * NF + 128), F32),
+            pltpu.VMEM((bulk * channels, 2 * NF + 128), F32),
+            pltpu.VMEM((bulk * channels, 2 * NF + 128), F32),
             pltpu.VMEM(table.shape, BF16),
             pltpu.SemaphoreType.DMA((3 * halves + 1,)),
         ],
@@ -470,6 +481,7 @@
             out_specs=vmem,
             scratch_shapes=[
                 pltpu.VMEM((NPART, features), BF16),
+                pltpu.VMEM((features, NPART), BF16),
                 pltpu.VMEM((lags * channels, NPART), F32),
             ],
             compiler_params=params,

time: 41.7 us -> 41.7 us (level)
  no operation moved by 1% of the time
where the time goes in v3:
time: 41.7 us; the launch traced here: 41.5 us
  Pallas kernels  20.9 us (50%)
  starting transfers between devices  11.6 us (28%)
  waiting for transfers between devices  7.94 us (19%)
  local copies, waits for them, and re-layouts  0.99 us (2%)
    ppermute x9, starting transfers between devices, exchange(): return lax.ppermute(value, 'chan', pairs)  11.6 us
    pallas_call x1, Pallas kernels, local(): pl.pallas_call(functools.partial(spectra_kernel, halves, own, halo), name...  11.1 us
    ppermute x9, waiting for transfers between devices, exchange(): return lax.ppermute(value, 'chan', pairs)  7.94 us
    pallas_call x2, Pallas kernels, product(): pl.pallas_call(functools.partial(product_kernel, late, chan_count, norm_s...  6.11 us
    pallas_call x1, Pallas kernels, local(): pl.pallas_call(functools.partial(rotate_kernel, lags), name='rotate', gri...  3.66 us
    unnamed x8, local copies, waits for them, and re-layouts  0.99 us
  transfers between devices with their start and end apart: 9, of which 5 were waited for; matrix products, arithmetic and copies ran while one was open for 0% of the time, Pallas kernels for 15%

profile of v3, /device:TPU:0, one launch (start us, length us, event | category | flops | bytes accessed | tf_op | source)
XLA Modules:
  0.0 41.5 jit_solution(14395924447910187058)
XLA Ops:
  0.0 0.0 copy-start.2
  0.0 0.0 copy-start.3
  0.0 11.1 %spectra.1.own.refs_0_ = bf16[32,4096]{1,0:T(8,128)(2,1)} custom-call(s32[32]{0:T(128)} %dead.1, s32[8]{0:T(128)} %offs, f32[32,32768]{1,0:T(8,128)} %x_hbm.1, bf16[512,1152]{1,0:T(8,128)(2,1)} %constant.30.clone.table_hbm), custom_call_target="tpu_custom_call" | custom-call | flops 7000000000 | bytes 8388608 | tf_op jit(solution)/shard_map/spectra/pallas_call | solution.py:423
  11.1 5.1 %collective-permute-start = (bf16[32,4096]{1,0:T(8,128)(2,1)}, bf16[32,4096]{1,0:T(8,128)(2,1)S(1)}, u32[]{:S(2)}, u32[]{:S(2)}) collective-permute-start(bf16[32,4096]{1,0:T(8,128)(2,1)} %spectra.1.own.refs_0_), channel_id=1, source_target_pairs={{0,12},{1,13},{2,14},{3,15},{4,0},{5,1},{6,2},{7,3},{8,4},{9,5},{1... | collective-permute-start | bytes 786440 | tf_op jit(solution)/shard_map/ppermute | solution.py:391
  16.2 0.0 copy-done.2
  16.2 0.0 copy-done.3
  16.2 0.0 copy-start
  16.2 1.0 %copy-done = bf16[32,4096]{1,0:T(8,128)(2,1)S(1)} copy-done((bf16[32,4096]{1,0:T(8,128)(2,1)S(1)}, bf16[32,4096]{1,0:T(8,128)(2,1)}, u32[]{:S(2)}) %copy-start) | copy-done | bytes 262168
  17.2 0.0 copy-start.1
  17.2 3.7 %rotate.1.rotated = bf16[1024,4096]{1,0:T(8,128)(2,1)S(1)} custom-call(bf16[32,4096]{1,0:T(8,128)(2,1)S(1)} %copy-done, f32[32,256]{1,0:T(8,128)S(1)} %copy-done.3, f32[32,256]{1,0:T(8,128)S(1)} %copy-done.2), custom_call_target="tpu_custom_call" | custom-call | flops 4000000000 | bytes 8388608 | tf_op jit(solution)/shard_map/rotate/pallas_call | solution.py:456
  20.9 1.2 %collective-permute-done.refs_1_ = bf16[32,4096]{1,0:T(8,128)(2,1)S(1)} collective-permute-done((bf16[32,4096]{1,0:T(8,128)(2,1)}, bf16[32,4096]{1,0:T(8,128)(2,1)S(1)}, u32[]{:S(2)}, u32[]{:S(2)}) %collective-permute-start) | collective-permute-done | bytes 262176 | tf_op jit(solution)/shard_map/ppermute | solution.py:391
  22.2 2.3 %collective-permute-start.1 = (bf16[32,4096]{1,0:T(8,128)(2,1)S(1)}, bf16[32,4096]{1,0:T(8,128)(2,1)S(1)}, u32[]{:S(2)}, u32[]{:S(2)}) collective-permute-start(bf16[32,4096]{1,0:T(8,128)(2,1)S(1)} %broadcast_select_fusion), channel_id=1, source_target_pairs={{0,10},{1,11},{2,0},{3,1},{4,2},{5,3},{6,4},{7,5},{8,6},{9,7},{10,... | collective-permute-start | bytes 786440 | tf_op jit(solution)/shard_map/ppermute | solution.py:391
  24.5 2.4 %collective-permute-start.5 = (bf16[32,4096]{1,0:T(8,128)(2,1)S(1)}, bf16[32,4096]{1,0:T(8,128)(2,1)S(1)}, u32[]{:S(2)}, u32[]{:S(2)}) collective-permute-start(bf16[32,4096]{1,0:T(8,128)(2,1)S(1)} %collective-permute-done.refs_1_), channel_id=1, source_target_pairs={{0,8},{1,9},{2,10},{3,11},{4,0},{5,1},{6,2},{7,3},{8,4},{9,5},{10,... | collective-permute-start | bytes 786440 | tf_op jit(solution)/shard_map/ppermute | solution.py:391
  26.9 0.7 %collective-permute-start.2 = (bf16[32,4096]{1,0:T(8,128)(2,1)S(1)}, bf16[32,4096]{1,0:T(8,128)(2,1)S(1)}, u32[]{:S(2)}, u32[]{:S(2)}) collective-permute-start(bf16[32,4096]{1,0:T(8,128)(2,1)S(1)} %collective-permute-done.refs_1_), channel_id=1, source_target_pairs={{0,2},{1,3},{2,0},{3,1},{4,6},{5,7},{6,4},{7,5},{8,10},{9,11},{10,... | collective-permute-start | bytes 786440 | tf_op jit(solution)/shard_map/ppermute | solution.py:391
  27.6 0.0 copy-done.1
  27.6 2.5 %early_product.1.refs_0_ = f32[1024,256]{1,0:T(8,128)S(1)} custom-call(s32[1]{0:T(128)} %bitcast.place, bf16[1024,4096]{1,0:T(8,128)(2,1)S(1)} %rotate.1.rotated, bf16[32,4096]{1,0:T(8,128)(2,1)S(1)} %copy-done.1, bf16[32,4096]{1,0:T(8,128)(2,1)S(1)} %collective-permute-done.refs_1_), custom_call_target="tpu_custom_call" | custom-call | flops 2147483648 | bytes 6291456 | tf_op jit(solution)/shard_map/early_product/pallas_call | solution.py:476
  30.0 1.2 %collective-permute-done.1.refs_7_ = bf16[32,4096]{1,0:T(8,128)(2,1)S(1)} collective-permute-done((bf16[32,4096]{1,0:T(8,128)(2,1)S(1)}, bf16[32,4096]{1,0:T(8,128)(2,1)S(1)}, u32[]{:S(2)}, u32[]{:S(2)}) %collective-permute-start.1) | collective-permute-done | bytes 262176 | tf_op jit(solution)/shard_map/ppermute | solution.py:391
  31.3 0.0 collective-permute-start.3
  31.3 0.5 %collective-permute-start.4 = (bf16[32,4096]{1,0:T(8,128)(2,1)S(1)}, bf16[32,4096]{1,0:T(8,128)(2,1)S(1)}, u32[]{:S(2)}, u32[]{:S(2)}) collective-permute-start(bf16[32,4096]{1,0:T(8,128)(2,1)S(1)} %collective-permute-done.refs_1_), channel_id=1, source_target_pairs={{0,1},{1,0},{2,3},{3,2},{4,5},{5,4},{6,7},{7,6},{8,9},{9,8},{10,11... | collective-permute-start | bytes 786440 | tf_op jit(solution)/shard_map/ppermute | solution.py:391
  31.8 0.0 collective-permute-start.8
  31.8 4.1 %collective-permute-done.5.refs_3_ = bf16[32,4096]{1,0:T(8,128)(2,1)S(1)} collective-permute-done((bf16[32,4096]{1,0:T(8,128)(2,1)S(1)}, bf16[32,4096]{1,0:T(8,128)(2,1)S(1)}, u32[]{:S(2)}, u32[]{:S(2)}) %collective-permute-start.5) | collective-permute-done | bytes 262176 | tf_op jit(solution)/shard_map/ppermute | solution.py:391
  35.9 0.0 collective-permute-start.6
  35.9 0.0 collective-permute-done.2.refs_5_
  35.9 0.0 collective-permute-done.3.refs_1_
  35.9 0.0 collective-permute-done.4.refs_2_
  35.9 0.6 %collective-permute-start.7 = (bf16[32,4096]{1,0:T(8,128)(2,1)S(1)}, bf16[32,4096]{1,0:T(8,128)(2,1)S(1)}, u32[]{:S(2)}, u32[]{:S(2)}) collective-permute-start(bf16[32,4096]{1,0:T(8,128)(2,1)S(1)} %collective-permute-done.2.refs_5_), channel_id=1, source_target_pairs={{0,1},{1,0},{2,3},{3,2},{4,5},{5,4},{6,7},{7,6},{8,9},{9,8},{10,11... | collective-permute-start | bytes 786440 | tf_op jit(solution)/shard_map/ppermute | solution.py:391
  36.5 0.9 %collective-permute-done.6.refs_4_ = bf16[32,4096]{1,0:T(8,128)(2,1)S(1)} collective-permute-done((bf16[32,4096]{1,0:T(8,128)(2,1)S(1)}, bf16[32,4096]{1,0:T(8,128)(2,1)S(1)}, u32[]{:S(2)}, u32[]{:S(2)}) %collective-permute-start.6) | collective-permute-done | bytes 262176 | tf_op jit(solution)/shard_map/ppermute | solution.py:391
  37.5 0.0 collective-permute-done.8.refs_8_
  37.5 0.4 collective-permute-done.7.refs_6_
  37.8 3.6 %late_product.1 = bf16[1024,256]{1,0:T(8,128)(2,1)} custom-call(s32[1]{0:T(128)} %bitcast.place, bf16[1024,4096]{1,0:T(8,128)(2,1)S(1)} %rotate.1.rotated, f32[1024,256]{1,0:T(8,128)S(1)} %early_product.1.refs_0_, bf16[32,4096]{1,0:T(8,128)(2,1)S(1)} %collective-permute-done.3.refs_1_, bf16[32,4096]{1,0:T(8,128)(2,1)S(1)} %collective-permute-done.4.refs_2_, ...), custom_call_target="tpu_custom_call" | custom-call | flops 2147483648 | bytes 6291456 | tf_op jit(solution)/shard_map/late_product/pallas_call | solution.py:476
  (1 shorter events, 0.0 us)
Async XLA Ops:
  0.0 16.2 %copy-start.2 = (f32[32,256]{1,0:T(8,128)S(1)}, f32[32,256]{1,0:T(8,128)}, u32[]{:S(2)}) copy-start(f32[32,256]{1,0:T(8,128)} %constant.32.clone.sin_lag) | copy-start | bytes 98308
  0.0 16.2 %copy-start.3 = (f32[32,256]{1,0:T(8,128)S(1)}, f32[32,256]{1,0:T(8,128)}, u32[]{:S(2)}) copy-start(f32[32,256]{1,0:T(8,128)} %constant.31.clone.cos_lag) | copy-start | bytes 98308
  11.1 11.0 %collective-permute-start = (bf16[32,4096]{1,0:T(8,128)(2,1)}, bf16[32,4096]{1,0:T(8,128)(2,1)S(1)}, u32[]{:S(2)}, u32[]{:S(2)}) collective-permute-start(bf16[32,4096]{1,0:T(8,128)(2,1)} %spectra.1.own.refs_0_), channel_id=1, source_target_pairs={{0,12},{1,13},{2,14},{3,15},{4,0},{5,1},{6,2},{7,3},{8,4},{9,5},{1... | collective-permute-start | bytes 786440 | tf_op jit(solution)/shard_map/ppermute | solution.py:391
  16.2 1.0 %copy-start = (bf16[32,4096]{1,0:T(8,128)(2,1)S(1)}, bf16[32,4096]{1,0:T(8,128)(2,1)}, u32[]{:S(2)}) copy-start(bf16[32,4096]{1,0:T(8,128)(2,1)} %spectra.1.own.refs_0_) | copy-start | bytes 786436
  17.2 10.3 %copy-start.1 = (bf16[32,4096]{1,0:T(8,128)(2,1)S(1)}, bf16[32,4096]{1,0:T(8,128)(2,1)}, u32[]{:S(2)}) copy-start(bf16[32,4096]{1,0:T(8,128)(2,1)} %spectra.1.own.refs_0_) | copy-start | bytes 786436
  22.2 9.1 %collective-permute-start.1 = (bf16[32,4096]{1,0:T(8,128)(2,1)S(1)}, bf16[32,4096]{1,0:T(8,128)(2,1)S(1)}, u32[]{:S(2)}, u32[]{:S(2)}) collective-permute-start(bf16[32,4096]{1,0:T(8,128)(2,1)S(1)} %broadcast_select_fusion), channel_id=1, source_target_pairs={{0,10},{1,11},{2,0},{3,1},{4,2},{5,3},{6,4},{7,5},{8,6},{9,7},{10,... | collective-permute-start | bytes 786440 | tf_op jit(solution)/shard_map/ppermute | solution.py:391
  24.5 11.4 %collective-permute-start.5 = (bf16[32,4096]{1,0:T(8,128)(2,1)S(1)}, bf16[32,4096]{1,0:T(8,128)(2,1)S(1)}, u32[]{:S(2)}, u32[]{:S(2)}) collective-permute-start(bf16[32,4096]{1,0:T(8,128)(2,1)S(1)} %collective-permute-done.refs_1_), channel_id=1, source_target_pairs={{0,8},{1,9},{2,10},{3,11},{4,0},{5,1},{6,2},{7,3},{8,4},{9,5},{10,... | collective-permute-start | bytes 786440 | tf_op jit(solution)/shard_map/ppermute | solution.py:391
  26.9 9.1 %collective-permute-start.2 = (bf16[32,4096]{1,0:T(8,128)(2,1)S(1)}, bf16[32,4096]{1,0:T(8,128)(2,1)S(1)}, u32[]{:S(2)}, u32[]{:S(2)}) collective-permute-start(bf16[32,4096]{1,0:T(8,128)(2,1)S(1)} %collective-permute-done.refs_1_), channel_id=1, source_target_pairs={{0,2},{1,3},{2,0},{3,1},{4,6},{5,7},{6,4},{7,5},{8,10},{9,11},{10,... | collective-permute-start | bytes 786440 | tf_op jit(solution)/shard_map/ppermute | solution.py:391
  31.3 4.7 %collective-permute-start.3 = (bf16[32,4096]{1,0:T(8,128)(2,1)S(1)}, bf16[32,4096]{1,0:T(8,128)(2,1)S(1)}, u32[]{:S(2)}, u32[]{:S(2)}) collective-permute-start(bf16[32,4096]{1,0:T(8,128)(2,1)S(1)} %copy-done.1), channel_id=1, source_target_pairs={{0,1},{1,0},{2,3},{3,2},{4,5},{5,4},{6,7},{7,6},{8,9},{9,8},{10,11... | collective-permute-start | bytes 786440 | tf_op jit(solution)/shard_map/ppermute | solution.py:391
  31.3 4.7 %collective-permute-start.4 = (bf16[32,4096]{1,0:T(8,128)(2,1)S(1)}, bf16[32,4096]{1,0:T(8,128)(2,1)S(1)}, u32[]{:S(2)}, u32[]{:S(2)}) collective-permute-start(bf16[32,4096]{1,0:T(8,128)(2,1)S(1)} %collective-permute-done.refs_1_), channel_id=1, source_target_pairs={{0,1},{1,0},{2,3},{3,2},{4,5},{5,4},{6,7},{7,6},{8,9},{9,8},{10,11... | collective-permute-start | bytes 786440 | tf_op jit(solution)/shard_map/ppermute | solution.py:391
  31.8 5.7 %collective-permute-start.8 = (bf16[32,4096]{1,0:T(8,128)(2,1)S(1)}, bf16[32,4096]{1,0:T(8,128)(2,1)S(1)}, u32[]{:S(2)}, u32[]{:S(2)}) collective-permute-start(bf16[32,4096]{1,0:T(8,128)(2,1)S(1)} %collective-permute-done.1.refs_7_), channel_id=1, source_target_pairs={{0,1},{1,0},{2,3},{3,2},{4,5},{5,4},{6,7},{7,6},{8,9},{9,8},{10,11... | collective-permute-start | bytes 786440 | tf_op jit(solution)/shard_map/ppermute | solution.py:391
  35.9 1.5 %collective-permute-start.6 = (bf16[32,4096]{1,0:T(8,128)(2,1)S(1)}, bf16[32,4096]{1,0:T(8,128)(2,1)S(1)}, u32[]{:S(2)}, u32[]{:S(2)}) collective-permute-start(bf16[32,4096]{1,0:T(8,128)(2,1)S(1)} %collective-permute-done.5.refs_3_), channel_id=1, source_target_pairs={{0,1},{1,0},{2,3},{3,2},{4,5},{5,4},{6,7},{7,6},{8,9},{9,8},{10,11... | collective-permute-start | bytes 786440 | tf_op jit(solution)/shard_map/ppermute | solution.py:391
  35.9 1.9 %collective-permute-start.7 = (bf16[32,4096]{1,0:T(8,128)(2,1)S(1)}, bf16[32,4096]{1,0:T(8,128)(2,1)S(1)}, u32[]{:S(2)}, u32[]{:S(2)}) collective-permute-start(bf16[32,4096]{1,0:T(8,128)(2,1)S(1)} %collective-permute-done.2.refs_5_), channel_id=1, source_target_pairs={{0,1},{1,0},{2,3},{3,2},{4,5},{5,4},{6,7},{7,6},{8,9},{9,8},{10,11... | collective-permute-start | bytes 786440 | tf_op jit(solution)/shard_map/ppermute | solution.py:391
